TPU v7x, 32 devices: a whole 2x2x4 slice. The times are simulated.
32 devices in a mesh: group: 2 (over y), gx: 4 (over z), gy: 2 (over x), gz: 2 (over core).
Axes of the slice: x: 2, y: 2, z: 4, core: 2. Of those that a mesh axis runs over, the one named last changes fastest.
Arguments:
- species: int32 [8, 2, 2, 216], P(('group', 'gx'), 'gy', 'gz'), parts along dimension 0, may hold values from 0 to 5
- counts: int32 [8, 2, 2], P(('group', 'gx'), 'gy', 'gz'), parts along dimension 0, may hold values from 27 to 216, as said below
- positions: float32 [8, 2, 2, 3, 216], P(('group', 'gx'), 'gy', 'gz'), parts along dimension 0, may hold values from 0 to 15, as said below
- ghost_rows: int32 [8, 2, 2, 152], P(('group', 'gx'), 'gy', 'gz'), parts along dimension 0, may hold values from 0 to 215, as said below
- neighbours: int32 [8, 2, 2, 26, 216], P(('group', 'gx'), 'gy', 'gz'), parts along dimension 0, may hold values from 0 to 727, as said below
- kvec: int32 [3, 4096], replicated, may hold values from -4 to 8, as said below
- embed: float32 [6, 64], replicated, may hold values from -6 to 6
- radial_one: float32 [8, 64], replicated, may hold values from -2 to 2
- radial_two: float32 [8, 64], replicated, may hold values from -2 to 2
- mix_one: float32 [64, 64], replicated, may hold values from -0.75 to 0.75
- mix_two: float32 [64, 64], replicated, may hold values from -0.75 to 0.75
- lr_filter: float32 [64, 4096], replicated, may hold values from -6 to 6
- read_weight: float32 [64, 64], replicated, may hold values from -0.75 to 0.75
- read_bias: float32 [64], replicated, may hold values from -3 to 3
- energy_weight: float32 [64], replicated, may hold values from -0.75 to 0.75
Outputs:
- energies: float32 [8, 2, 2, 216], P(('group', 'gx'), 'gy', 'gz'), parts along dimension 0
- forces: float32 [8, 2, 2, 3, 216], P(('group', 'gx'), 'gy', 'gz'), parts along dimension 0
There are 2 independent parts, one for each index of `group`. A program takes and returns all parts, laid end to end along the dimension named above; an argument that names none is the same for every part. Nothing has to cross between parts.
Inputs may be any that keep to these rules, and one draw needn't show every extreme that they name: `counts`: every draw has a domain with 216 live slots and one with 27. `positions`: each slot of a domain sits at one site, each site holds one slot; each coordinate of an atom lies within 0.625 of its site's centre 2.5 * (s + 0.5). ghost_rows[x, y, z, g] is the slot at the g-th boundary site of the domain. `neighbours`: for a slot at site s, m runs over the 26 sites s + o with each o_d -1, 0 or 1, not all 0, in increasing order of (ox, oy, oz); a site inside the domain is named by its slot, one outside by 216 plus its extended-grid cell number. `kvec`: row 0 is 1 to 8; rows 1 and 2 are at most 4 and 4 in magnitude; each bound is reached.
All inputs are finite; a program needn't handle non-finite values.
Results may differ from a plain program's by a relative error of at most 0.0057.
Values may be sent and summed in bfloat16 or wider, within the bound.
No kernel may reach another device: no remote copies, remote signals or barrier semaphores. Data moves between devices by JAX's collectives and lax.ppermute only.
A program may use at most 128 MiB of HBM per device.

v0:
```python
import math

import jax
import jax.numpy as jnp
import numpy as np
from jax import lax
from jax.experimental import pallas as pl
from jax.experimental.pallas import tpu as pltpu
from jax.sharding import PartitionSpec as P

SIDE = 6
KVEC = 4096
NBASIS = 8
NEIGH = 26


spacing = 2.5
cutoff = 5.0
two_pi = 6.283185307179586
highest = lax.Precision.HIGHEST


def passed_along(block, axis, distance):
    devices = range(lax.axis_size(axis))
    route = [((i - distance) % len(devices), i) for i in devices]
    return lax.ppermute(block, axis, route)


def extended(block, sides, width):
    for axis, dim in sides:
        count = lax.axis_size(axis)
        forward = [(i, i + 1) for i in range(count - 1)]
        forward.append((count - 1, 0))
        backward = [(target, source) for source, target in forward]
        low = lax.ppermute(
            lax.slice_in_dim(block, block.shape[dim] - width, None, axis=dim), axis, forward
        )
        high = lax.ppermute(lax.slice_in_dim(block, 0, width, axis=dim), axis, backward)
        block = jnp.concatenate([low, block, high], axis=dim)
    return block


def rows_per_block():
    return SIDE * SIDE


def boundary_list(side):
    site_ids = np.arange(side**3).reshape(side, side, side)
    inner = np.zeros((side, side, side), dtype=bool)
    inner[1 : side - 1, 1 : side - 1, 1 : side - 1] = True
    return site_ids[~inner].astype(np.int32)


def radial_terms(distance):
    centres = cutoff * jnp.arange(NBASIS).astype(jnp.float32) / (NBASIS - 1)
    sharpness = (NBASIS / cutoff) ** 2
    gap_value = distance[None] - centres[:, None, None]
    gaussian = jnp.exp(-sharpness * gap_value * gap_value)
    envelope_base = jnp.maximum(1.0 - distance * distance / (cutoff * cutoff), 0.0)
    envelope = envelope_base * envelope_base
    envelope_slope = -4.0 * distance * envelope_base / (cutoff * cutoff)
    radial_value = gaussian * envelope[None]
    radial_slope = gaussian * (envelope_slope[None] - 2.0 * sharpness * gap_value * envelope[None])
    return (radial_value, radial_slope)


def embed_codes(type_code, embed):
    species_ids = jnp.arange(1, embed.shape[0] + 1, dtype=jnp.int32).astype(type_code.dtype)
    one_hot = (type_code[None, :] == species_ids[:, None]).astype(jnp.float32)
    return jnp.dot(embed.T, one_hot, precision=highest, preferred_element_type=jnp.float32)


def cell_shift():
    ext_side = SIDE + 2
    cells = jnp.arange(ext_side**3, dtype=jnp.int32)
    coords = jnp.stack(
        [cells // (ext_side * ext_side), cells // ext_side % ext_side, cells % ext_side]
    )
    domain_width = SIDE * spacing
    return jnp.where(
        coords == 0, -domain_width, jnp.where(coords == ext_side - 1, domain_width, 0.0)
    ).astype(jnp.float32)


def pair_geometry(coords_own, pool_coords, pair_lists):
    separation = jnp.take(pool_coords, pair_lists, axis=1) - coords_own[:, None, :]
    distance = jnp.sqrt(jnp.sum(separation * separation, axis=0))
    return (separation, distance)


def message_forward(pool_values, pair_lists, radial_value, radial_weight):
    radial_filter = jnp.einsum("bc,bma->cma", radial_weight, radial_value, precision=highest)
    neighbour_value = jnp.take(pool_values, pair_lists, axis=1)
    return jnp.sum(radial_filter * neighbour_value, axis=1)


def message_backward(
    grad_message,
    pool_values,
    pair_lists,
    radial_value,
    radial_slope,
    radial_weight,
    separation,
    distance,
    pool_size,
    with_features,
):
    neighbour_value = jnp.take(pool_values, pair_lists, axis=1)
    contracted = jnp.einsum(
        "bc,cma->bma", radial_weight, grad_message[:, None, :] * neighbour_value, precision=highest
    )
    energy_slope = jnp.sum(radial_slope * contracted, axis=0)
    pair_force = separation * (energy_slope / distance)[None]
    flat_index = pair_lists.reshape(-1)
    grad_pool = (
        jnp.zeros((3, pool_size), jnp.float32).at[:, flat_index].add(pair_force.reshape(3, -1))
    )
    grad_own = -jnp.sum(pair_force, axis=1)
    if with_features:
        radial_filter = jnp.einsum("bc,bma->cma", radial_weight, radial_value, precision=highest)
        spread = (radial_filter * grad_message[:, None, :]).reshape(radial_filter.shape[0], -1)
        feature_pool = (
            jnp.zeros((radial_filter.shape[0], pool_size), jnp.float32)
            .at[:, flat_index]
            .add(spread)
        )
        return (grad_pool, grad_own, feature_pool)
    return (grad_pool, grad_own, grad_pool)


def phase_table(fraction, wave_numbers):
    phase_angle = two_pi * (
        fraction[0][:, None] * wave_numbers[0][None, :]
        + fraction[1][:, None] * wave_numbers[1][None, :]
        + fraction[2][:, None] * wave_numbers[2][None, :]
    )
    return (jnp.cos(phase_angle).astype(jnp.bfloat16), jnp.sin(phase_angle).astype(jnp.bfloat16))


def read_long(cosine_low, sine_low, filtered):
    dims = (((1,), (1,)), ((), ()))
    return lax.dot_general(
        filtered[0], cosine_low, dims, preferred_element_type=jnp.float32
    ) + lax.dot_general(filtered[1], sine_low, dims, preferred_element_type=jnp.float32)


def block_live(step_index, live_count):
    block_rows = rows_per_block()
    per_member = SIDE**3 // block_rows
    first_row = (step_index % per_member * block_rows).astype(jnp.float32)
    return first_row < live_count[step_index // per_member]


def lr_struct(fraction, row_values, live_count, wave_numbers):
    block_rows = rows_per_block()
    blocks = fraction.shape[1] // block_rows

    def step(step_index, running):

        def work(running):
            offset = step_index * block_rows
            frac_block = lax.dynamic_slice_in_dim(fraction, offset, block_rows, 1)
            feature_block = lax.dynamic_slice_in_dim(row_values, offset, block_rows, 1)
            cosine_low, sine_low = phase_table(frac_block, wave_numbers)
            term = jnp.stack(
                [
                    jnp.dot(feature_block, cosine_low, preferred_element_type=jnp.float32),
                    jnp.dot(feature_block, sine_low, preferred_element_type=jnp.float32),
                ]
            )
            return running + term

        return lax.cond(
            block_live(step_index, live_count), work, lambda unchanged: unchanged, running
        )

    initial = jnp.zeros((2, row_values.shape[0], wave_numbers.shape[1]), jnp.float32)
    return lax.fori_loop(0, blocks, step, initial)


def lr_read(fraction, live_count, wave_numbers, filtered):
    block_rows = rows_per_block()
    blocks = fraction.shape[1] // block_rows

    def step(step_index, result):

        def work(result):
            offset = step_index * block_rows
            cosine_low, sine_low = phase_table(
                lax.dynamic_slice_in_dim(fraction, offset, block_rows, 1), wave_numbers
            )
            return lax.dynamic_update_slice_in_dim(
                result, read_long(cosine_low, sine_low, filtered), offset, 1
            )

        return lax.cond(
            block_live(step_index, live_count), work, lambda unchanged: unchanged, result
        )

    initial = jnp.zeros((filtered.shape[1], fraction.shape[1]), jnp.float32)
    return lax.fori_loop(0, blocks, step, initial)


def lr_back(
    fraction,
    rounded_rows,
    grad_rows,
    occupied_rows,
    live_count,
    wave_numbers,
    wave_factors,
    filtered,
    back_filtered,
):
    block_rows = rows_per_block()
    blocks = fraction.shape[1] // block_rows
    dims = (((0,), (0,)), ((), ()))
    right_real = jnp.concatenate([filtered[0], back_filtered[0]], axis=0)
    right_imag = jnp.concatenate([filtered[1], back_filtered[1]], axis=0)

    def step(step_index, carried):

        def work(carried):
            grad_long, force_long = carried
            offset = step_index * block_rows
            cosine_low, sine_low = phase_table(
                lax.dynamic_slice_in_dim(fraction, offset, block_rows, 1), wave_numbers
            )
            mask_block = lax.dynamic_slice_in_dim(occupied_rows, offset, block_rows, 0)
            grad_block = mask_block[None] * read_long(cosine_low, sine_low, back_filtered)
            stacked_left = jnp.concatenate(
                [
                    lax.dynamic_slice_in_dim(grad_rows, offset, block_rows, 1),
                    lax.dynamic_slice_in_dim(rounded_rows, offset, block_rows, 1),
                ],
                axis=0,
            )
            real_part = lax.dot_general(
                stacked_left, right_real, dims, preferred_element_type=jnp.float32
            )
            imag_part = lax.dot_general(
                stacked_left, right_imag, dims, preferred_element_type=jnp.float32
            )
            turning = (
                cosine_low.astype(jnp.float32) * imag_part
                - sine_low.astype(jnp.float32) * real_part
            )
            force_block = lax.dot_general(
                wave_factors,
                turning,
                (((1,), (1,)), ((), ())),
                precision=highest,
                preferred_element_type=jnp.float32,
            )
            return (
                lax.dynamic_update_slice_in_dim(grad_long, grad_block, offset, 1),
                lax.dynamic_update_slice_in_dim(force_long, force_block, offset, 1),
            )

        return lax.cond(
            block_live(step_index, live_count), work, lambda unchanged: unchanged, carried
        )

    initial = (
        jnp.zeros((rounded_rows.shape[0], fraction.shape[1]), jnp.float32),
        jnp.zeros((3, fraction.shape[1]), jnp.float32),
    )
    return lax.fori_loop(0, blocks, step, initial)


def boundary_grid(values, ghost_slots, boundary):
    picked = jnp.take(values, ghost_slots, axis=1)
    site_grid = jnp.zeros((values.shape[0], SIDE**3), values.dtype).at[:, boundary].set(picked)
    return site_grid.reshape(values.shape[0], SIDE, SIDE, SIDE)


def fold_slab(site_grid, axis_number, from_left, from_right):
    inner_size = site_grid.shape[axis_number] - 2
    inner = lax.slice_in_dim(site_grid, 1, inner_size + 1, axis=axis_number)
    first_layer = lax.slice_in_dim(inner, 0, 1, axis=axis_number) + from_left
    last_layer = lax.slice_in_dim(inner, inner_size - 1, inner_size, axis=axis_number) + from_right
    middle = lax.slice_in_dim(inner, 1, inner_size - 1, axis=axis_number)
    return jnp.concatenate([first_layer, middle, last_layer], axis=axis_number)


def return_halo(site_grid):
    edge = site_grid.shape[3] - 1
    received = [
        passed_along(
            lax.slice_in_dim(site_grid, slab_start, slab_start + 1, axis=3), "gz", direction
        )
        for direction, slab_start in ((1, edge), (-1, 0))
    ]
    site_grid = fold_slab(site_grid, 3, received[0], received[1])
    edge = site_grid.shape[2] - 1
    received = [
        passed_along(
            lax.slice_in_dim(site_grid, slab_start, slab_start + 1, axis=2), "gy", direction
        )
        for direction, slab_start in ((1, edge), (-1, 0))
    ]
    site_grid = fold_slab(site_grid, 2, received[0], received[1])
    edge = site_grid.shape[1] - 1
    received = [
        passed_along(
            lax.slice_in_dim(site_grid, slab_start, slab_start + 1, axis=1), "gx", direction
        )
        for direction, slab_start in ((1, edge), (-1, 0))
    ]
    return fold_slab(site_grid, 1, received[0], received[1])


def ghost_to_rows(site_grid, ghost_slots, boundary):
    features = site_grid.shape[0]
    picked = site_grid.reshape(features, -1)[:, boundary]
    return jnp.zeros((features, SIDE**3), site_grid.dtype).at[:, ghost_slots].add(picked)


def local(
    species,
    counts,
    positions,
    ghost_rows,
    neighbours,
    kvec,
    embed,
    radial_one,
    radial_two,
    mix_one,
    mix_two,
    lr_filter,
    read_weight,
    read_bias,
    energy_weight,
):
    slot_count = SIDE**3
    ext_side = SIDE + 2
    pool_size = slot_count + ext_side**3
    pair_scale = 1.0 / math.sqrt(NEIGH)
    domain_width = SIDE * spacing
    mesh_sizes = (lax.axis_size("gx"), lax.axis_size("gy"), lax.axis_size("gz"))
    box_length = tuple((count_along * domain_width for count_along in mesh_sizes))
    wave_scale = 1.0 / math.sqrt(
        KVEC * (slot_count * mesh_sizes[0] * mesh_sizes[1] * mesh_sizes[2])
    )
    species_flat = species.reshape(slot_count)
    live_total = counts.reshape(())
    coords_own = positions.reshape(3, slot_count)
    ghost_slots = ghost_rows.reshape(-1)
    pair_lists = neighbours.reshape(NEIGH, slot_count)
    boundary = jnp.asarray(boundary_list(SIDE))
    cell_offset = cell_shift()
    occupied = (jnp.arange(slot_count, dtype=jnp.int32) < live_total).astype(jnp.float32)
    type_code = jnp.where(occupied > 0, species_flat + 1, 0).astype(jnp.float32)
    hidden_zero = embed_codes(species_flat + 1, embed)
    masked_zero = hidden_zero * occupied[None]
    packet = boundary_grid(
        jnp.concatenate([coords_own, type_code[None]], axis=0), ghost_slots, boundary
    )
    ext_atoms = extended(packet, (("gx", 1), ("gy", 2), ("gz", 3)), 1).reshape(4, -1)
    pool_coords = jnp.concatenate([coords_own, ext_atoms[:3] + cell_offset], axis=1)
    pool_zero = jnp.concatenate([masked_zero, embed_codes(ext_atoms[3], embed)], axis=1)
    separation, distance = pair_geometry(coords_own, pool_coords, pair_lists)
    radial_value, radial_slope = radial_terms(distance)
    message = message_forward(pool_zero, pair_lists, radial_value, radial_one)
    hidden_one = hidden_zero + pair_scale * jnp.dot(
        mix_one.T, message, precision=highest, preferred_element_type=jnp.float32
    )
    masked_one = hidden_one * occupied[None]
    rounded_one = masked_one.astype(jnp.bfloat16)
    domain_pos = (lax.axis_index("gx"), lax.axis_index("gy"), lax.axis_index("gz"))
    fraction = jnp.stack(
        [
            (domain_pos[axis_id].astype(jnp.float32) * domain_width + coords_own[axis_id])
            / box_length[axis_id]
            for axis_id in range(3)
        ]
    )
    wave_numbers = kvec.astype(jnp.float32)
    wave_factors = jnp.stack(
        [two_pi * wave_numbers[axis_id] / box_length[axis_id] for axis_id in range(3)]
    )
    own_count = jnp.sum(occupied)[None]
    share_size = KVEC // (mesh_sizes[0] * mesh_sizes[1] * mesh_sizes[2])
    share_start = lax.axis_index(("gx", "gy", "gz")) * share_size
    filter_share = lax.dynamic_slice_in_dim(lr_filter, share_start, share_size, 1)
    struct_part = lax.psum_scatter(
        lr_struct(fraction, rounded_one, own_count, wave_numbers),
        ("gx", "gy", "gz"),
        scatter_dimension=2,
        tiled=True,
    )
    filtered = lax.all_gather(
        (struct_part * filter_share[None] * wave_scale).astype(jnp.bfloat16),
        ("gx", "gy", "gz"),
        axis=2,
        tiled=True,
    )
    long_part = lr_read(fraction, own_count, wave_numbers, filtered)
    masked_ext = extended(
        boundary_grid(masked_one, ghost_slots, boundary).astype(jnp.bfloat16),
        (("gx", 1), ("gy", 2), ("gz", 3)),
        1,
    ).astype(jnp.float32)
    pool_one = jnp.concatenate([masked_one, masked_ext.reshape(masked_one.shape[0], -1)], axis=1)
    message_two = message_forward(pool_one, pair_lists, radial_value, radial_two)
    hidden_two = (
        hidden_one
        + pair_scale
        * jnp.dot(mix_two.T, message_two, precision=highest, preferred_element_type=jnp.float32)
        + long_part
    )
    activation = (
        jnp.dot(read_weight.T, hidden_two, precision=highest, preferred_element_type=jnp.float32)
        + read_bias[:, None]
    )
    gating = jax.nn.sigmoid(activation)
    energies = occupied * jnp.sum(activation * gating * energy_weight[:, None], axis=0)
    grad_act = (
        occupied[None] * energy_weight[:, None] * gating * (1.0 + activation * (1.0 - gating))
    )
    grad_two = jnp.dot(read_weight, grad_act, precision=highest, preferred_element_type=jnp.float32)
    grad_low = grad_two.astype(jnp.bfloat16)
    grad_part = lax.psum_scatter(
        lr_struct(fraction, grad_low, own_count, wave_numbers),
        ("gx", "gy", "gz"),
        scatter_dimension=2,
        tiled=True,
    )
    back_filtered = lax.all_gather(
        (grad_part * filter_share[None] * wave_scale).astype(jnp.bfloat16),
        ("gx", "gy", "gz"),
        axis=2,
        tiled=True,
    )
    grad_long, force_long = lr_back(
        fraction,
        rounded_one,
        grad_low,
        occupied,
        own_count,
        wave_numbers,
        wave_factors,
        filtered,
        back_filtered,
    )
    grad_message = pair_scale * jnp.dot(
        mix_two, grad_two, precision=highest, preferred_element_type=jnp.float32
    )
    grad_pool, grad_own_two, feature_pool = message_backward(
        grad_message,
        pool_one,
        pair_lists,
        radial_value,
        radial_slope,
        radial_two,
        separation,
        distance,
        pool_size,
        True,
    )
    combined = jnp.concatenate([feature_pool, grad_pool], axis=0)
    features = combined.shape[0]
    returned_two = ghost_to_rows(
        return_halo(combined[:, slot_count:].reshape(features, ext_side, ext_side, ext_side)),
        ghost_slots,
        boundary,
    )
    own_two = combined[:, :slot_count]
    channels = masked_one.shape[0]
    grad_one = (
        grad_two + grad_long + occupied[None] * (own_two[:channels] + returned_two[:channels])
    )
    grad_message_one = pair_scale * jnp.dot(
        mix_one, grad_one, precision=highest, preferred_element_type=jnp.float32
    )
    grad_pool_one, grad_own_one, unused = message_backward(
        grad_message_one,
        pool_zero,
        pair_lists,
        radial_value,
        radial_slope,
        radial_one,
        separation,
        distance,
        pool_size,
        False,
    )
    layer_one_grad = grad_own_one + grad_pool_one[:, :slot_count]
    returned_one = ghost_to_rows(
        return_halo(grad_pool_one[:, slot_count:].reshape(3, ext_side, ext_side, ext_side)),
        ghost_slots,
        boundary,
    )
    total_grad = (
        layer_one_grad
        + returned_one
        + force_long
        + grad_own_two
        + own_two[channels:]
        + returned_two[channels:]
    )
    forces = -total_grad
    return (energies.reshape(1, 1, 1, slot_count), forces.reshape(1, 1, 1, 3, slot_count))


offsets = tuple(
    (ox, oy, oz)
    for ox in (0, 1)
    for oy in (-1, 0, 1)
    for oz in (-1, 0, 1)
    if (ox, oy, oz) > (0, 0, 0)
)
half = len(offsets)
slots = SIDE**3
ext = SIDE + 2
cells = ext**3
chan = 64
grid_dims = (4, 2, 2)
domains = 16
planes = 8
rows_all = slots * planes
waves = 648
table = 2 * waves
pad = 256
gamma = (NBASIS / cutoff) ** 2
step = cutoff / (NBASIS - 1)
nt = (((1,), (1,)), ((), ()))
nn = (((1,), (0,)), ((), ()))
f32 = jnp.float32
bf16 = jnp.bfloat16


def dot(left, right, dims=nn, precision=None):
    return lax.dot_general(left, right, dims, precision=precision, preferred_element_type=f32)


def split(value):
    high = value.astype(bf16)
    return high, (value - high.astype(f32)).astype(bf16)


def dot_split(left, high, low):
    left_high, left_low = split(left)
    return dot(left_high, high) + dot(left_low, high) + dot(left_high, low)


def site_of(coords):
    where = (coords * (1.0 / spacing)).astype(jnp.int32)
    return (where[0:1] * SIDE + where[1:2]) * SIDE + where[2:3]


def iota(shape, dim):
    return lax.broadcasted_iota(jnp.int32, shape, dim)


def place_kernel(count_ref, pos_ref, species_ref, out_ref):
    coords = pos_ref[...]
    live = iota((1, slots), 1) < count_ref[0]
    code = jnp.where(live, species_ref[...] + 1, 0).astype(f32)
    data = jnp.concatenate([coords, code], axis=0)
    hot = (iota((slots, slots), 0) == site_of(coords)).astype(f32)
    out_ref[...] = dot(data, hot, nt, highest)


def twice(block):
    zero = jnp.zeros_like(block)
    return jnp.concatenate(
        [jnp.concatenate([block, zero], axis=1), jnp.concatenate([zero, block], axis=1)], axis=0
    )


def weights_kernel(
    kvec_ref,
    filter_ref,
    embed_ref,
    one_ref,
    two_ref,
    mix_one_ref,
    mix_two_ref,
    read_ref,
    gain_ref,
    radial_ref,
    embed_out,
    mix_ref,
    act_ref,
    grad_ref,
    back_ref,
    pair_ref,
):
    pair_scale = 1.0 / math.sqrt(NEIGH)
    wave_scale = 1.0 / math.sqrt(KVEC * slots * domains)
    waves_in = kvec_ref[...]

    def folded(row):
        return jnp.where(row > 0, 2 * row - 1, -2 * row)

    index = (folded(waves_in[1:2]) * 9 + folded(waves_in[2:3])) * 8 + waves_in[0:1] - 1
    filter_high, filter_low = split(filter_ref[...] * wave_scale)
    parts = jnp.concatenate([filter_high, filter_low], axis=0)
    gain = jnp.zeros((waves, 2 * chan), f32)
    width = 1024
    for start in range(0, KVEC, width):
        hot = (iota((waves, width), 0) == index[:, start : start + width]).astype(f32).astype(bf16)
        gain = gain + dot(hot, parts[:, start : start + width], nt)
    gain = (gain[:, :chan] + gain[:, chan:]).reshape(waves // 8, 8, chan)
    gain_ref[...] = jnp.concatenate([gain, gain], axis=1).reshape(table, chan)

    centre = step * iota((NBASIS, 1), 0).astype(f32)
    fall = jnp.exp(-gamma * centre * centre)
    rows = iota((pad, pad), 0)
    columns = iota((pad, pad), 1)
    kept = (rows // 128) == (columns % 128 // chan)

    def spread(block):
        return jnp.broadcast_to(block[:, None, :], (NBASIS, 16, chan)).reshape(128, chan)

    def wide(left, right):
        left, right = spread(left), spread(right)
        line = jnp.concatenate([left, left, right, right], axis=1)
        return jnp.concatenate([line, line], axis=0)

    radial = wide(one_ref[...] * fall, two_ref[...] * fall)
    for offset in range(half):
        radial_ref[offset] = jnp.where(kept & (rows % 16 == offset), radial, 0.0).astype(bf16)
    table_rows = jnp.concatenate([embed_ref[...], jnp.zeros((2, chan), f32)], axis=0)
    high = table_rows.astype(bf16).astype(f32)
    species_rows = kept & (rows % 16 == half)
    embeds = jnp.where(species_rows, wide(high, table_rows - high), 0.0).astype(bf16)
    lives = jnp.where(species_rows[:, :128], 1.0, 0.0).astype(bf16)
    embed_out[...] = jnp.concatenate([embeds, lives], axis=1)

    def put(ref, value):
        value_high, value_low = split(value)
        ref[0] = value_high
        ref[1] = value_low

    mix_two = mix_two_ref[...]
    read = read_ref[...]
    both = dot(mix_two, read, nn, highest) * pair_scale
    put(mix_ref, twice(mix_one_ref[...] * pair_scale))
    put(act_ref, jnp.concatenate([twice(read), twice(both)], axis=0))
    put(grad_ref, jnp.concatenate([twice(read.T), twice(both.T)], axis=1))
    put(back_ref, mix_one_ref[...].T * pair_scale)
    pairs = jnp.concatenate([two_ref[...], two_ref[...], one_ref[...], one_ref[...]], axis=1)
    pairs_high = pairs.astype(bf16).astype(f32)
    pair_ref[...] = jnp.concatenate([pairs_high, pairs - pairs_high], axis=0).astype(bf16)


def turn(fraction):
    rest = fraction - jnp.floor(fraction + 0.5)
    angle = rest * (0.5 * two_pi)
    square = angle * angle
    sine = angle * (
        1.0
        + square
        * (
            -1.0 / 6
            + square
            * (
                1.0 / 120
                + square * (-1.0 / 5040 + square * (1.0 / 362880 - square * (1.0 / 39916800)))
            )
        )
    )
    cosine = 1.0 + square * (
        -0.5
        + square
        * (
            1.0 / 24
            + square
            * (
                -1.0 / 720
                + square
                * (1.0 / 40320 + square * (-1.0 / 3628800 + square * (1.0 / 479001600)))
            )
        )
    )
    return 1.0 - 2.0 * sine * sine, 2.0 * sine * cosine


def fan(base, step_pairs):
    real, imag = base
    out = [(real, imag)]
    for cosine, sine in step_pairs:
        a, b, c, d = real * cosine, imag * sine, real * sine, imag * cosine
        out.append((a - b, c + d))
        out.append((a + b, d - c))
    return out


def wave_tile(coords, store):
    frac = [coords[axis] / (grid_dims[axis] * SIDE * spacing) for axis in range(3)]
    row = iota((8, 128), 0)
    base = turn(frac[0] * (row + 1).astype(f32))
    rest = turn(jnp.where(row < 4, frac[1], frac[2]) * (row % 4 + 1).astype(f32))

    def line(index):
        return tuple(jnp.broadcast_to(part[index : index + 1], (8, 128)) for part in rest)

    y_lines = [line(index) for index in range(4)]
    z_lines = [line(index + 4) for index in range(4)]
    index = 0
    for level in fan(base, y_lines):
        for real, imag in fan(level, z_lines):
            store(index, jnp.concatenate([real, imag], axis=0).astype(bf16))
            index += 1


def swap_lanes(value):
    return pltpu.roll(value, chan, value.ndim - 1)


def swap_planes(value):
    up = pltpu.roll(value, 1, 1)
    down = pltpu.roll(value, planes - 1, 1)
    return jnp.where(iota(value.shape, 1) % 2 == 0, down, up)


def as_three(value):
    return value.reshape((-1,) + value.shape[-2:])


def fill_ghosts(ref):
    inner = slice(1, SIDE + 1)
    for ghost, source, shift in ((0, SIDE, 2), (SIDE + 1, 1, planes - 2)):
        value = ref[source, inner, inner]
        ref[ghost, inner, inner] = pltpu.roll(as_three(value), shift, 1).reshape(value.shape)
    for ghost, source in ((0, SIDE), (SIDE + 1, 1)):
        value = ref[:, source, inner]
        ref[:, ghost, inner] = swap_planes(as_three(value)).reshape(value.shape)
    for ghost, source in ((0, SIDE), (SIDE + 1, 1)):
        value = ref[:, :, source]
        ref[:, :, ghost] = swap_lanes(as_three(value)).reshape(value.shape)


def fold_ghosts(ref):
    inner = slice(1, SIDE + 1)
    for ghost, target in ((SIDE + 1, 1), (0, SIDE)):
        value = ref[:, :, ghost]
        ref[:, :, target] = ref[:, :, target] + swap_lanes(as_three(value)).reshape(value.shape)
    for ghost, target in ((SIDE + 1, 1), (0, SIDE)):
        value = ref[:, ghost, inner]
        ref[:, target, inner] = ref[:, target, inner] + swap_planes(as_three(value)).reshape(
            value.shape
        )
    for ghost, target, shift in ((SIDE + 1, 1, 2), (0, SIDE, planes - 2)):
        value = ref[ghost, inner, inner]
        ref[target, inner, inner] = ref[target, inner, inner] + pltpu.roll(
            as_three(value), shift, 1
        ).reshape(value.shape)


def inner_rows(ref):
    inner = slice(1, SIDE + 1)
    return ref[inner, inner, inner].reshape(rows_all, 128)


def set_inner(ref, value):
    inner = slice(1, SIDE + 1)
    ref[inner, inner, inner] = value.reshape(SIDE, SIDE, SIDE, planes, 128)


def convolve(filters, layer, source, target):
    target[...] = jnp.zeros(target.shape, f32)
    lanes = slice(layer * 128, layer * 128 + 128)
    groups = {}
    for number, (ox, oy, oz) in enumerate(offsets):
        groups.setdefault((ox, oy), []).append((number, oz))

    def body(line, carry):
        x = line // SIDE
        y = line % SIDE
        own = [source[x + 1, y + 1, z + 1] for z in range(SIDE)]
        own_sum = [jnp.zeros((planes, 128), f32)] * SIDE
        for (ox, oy), members in groups.items():
            there = [source[x + 1 + ox, y + 1 + oy, z] for z in range(ext)]
            sums = [None] * ext
            for z in range(SIDE):
                for number, oz in members:
                    first = pl.multiple_of((line * SIDE + z) * planes, planes)
                    weight = filters[number, pl.ds(first, planes), lanes]
                    own_sum[z] = own_sum[z] + weight * there[z + 1 + oz]
                    term = weight * own[z]
                    spot = z + 1 + oz
                    sums[spot] = term if sums[spot] is None else sums[spot] + term
            for z in range(ext):
                if sums[z] is not None:
                    target[x + 1 + ox, y + 1 + oy, z] = target[x + 1 + ox, y + 1 + oy, z] + sums[z]
        for z in range(SIDE):
            target[x + 1, y + 1, z + 1] = target[x + 1, y + 1, z + 1] + own_sum[z]
        return carry

    lax.fori_loop(0, SIDE * SIDE, body, 0)
    fold_ghosts(target)


def box_kernel(
    place_ref,
    all_ref,
    pos_ref,
    gain_ref,
    radial_ref,
    embed_ref,
    mix_ref,
    act_ref,
    grad_ref,
    back_ref,
    pair_ref,
    bias_ref,
    energy_ref,
    out_ref,
    sep_ref,
    sites_ref,
    basis_ref,
    filters_ref,
    waves_ref,
    ring_ref,
    zero_ref,
    one_ref,
    two_ref,
    sum_ref,
    packed_ref,
    shift_ref,
    own_ref,
):
    home = [place_ref[axis] for axis in range(3)]
    sites_ref[...] = jnp.zeros((4 * domains, pad), f32)
    for number in range(domains):
        spot = [
            lax.rem(home[axis] + part, grid_dims[axis])
            for axis, part in enumerate((number // 4, number // 2 % 2, number % 2))
        ]
        sites_ref[number * 4 : number * 4 + 4, 0:slots] = all_ref[
            (spot[0] * 2 + spot[1]) * 2 + spot[2]
        ]
    sites = sites_ref[:, 0:slots]

    lane = iota((1, cells), 1)
    coords = [lane // (ext * ext), lane // ext % ext, lane % ext]
    wrapped = [(value + SIDE - 1) % SIDE for value in coords]
    wrapped_site = (wrapped[0] * SIDE + wrapped[1]) * SIDE + wrapped[2]
    inside = coords[0] >= 0
    for value in coords:
        inside = inside & (value > 0) & (value < ext - 1)
    hot_all = iota((slots, cells), 0) == wrapped_site
    grown = dot(sites, hot_all.astype(f32), nn, highest)
    picks = (hot_all & inside).astype(f32)

    back16 = jnp.concatenate([grown[48:], grown[:48]], axis=0)
    ahead16 = jnp.concatenate([grown[16:], grown[:16]], axis=0)
    grown = jnp.where(coords[0] == 0, back16, jnp.where(coords[0] == ext - 1, ahead16, grown))
    swapped = jnp.concatenate(
        [grown[8 * (part ^ 1) : 8 * (part ^ 1) + 8] for part in range(8)], axis=0
    )
    grown = jnp.where((coords[1] == 0) | (coords[1] == ext - 1), swapped, grown)
    swapped = pltpu.roll(grown.reshape(8, 8, cells), 4, 1).reshape(64, cells)
    grown = jnp.where((coords[2] == 0) | (coords[2] == ext - 1), swapped, grown)
    component = iota((64, cells), 0) % 4
    domain_width = SIDE * spacing
    for axis in range(3):
        moved = jnp.where(
            coords[axis] == 0,
            -domain_width,
            jnp.where(coords[axis] == ext - 1, domain_width, 0.0),
        )
        grown = grown + jnp.where(component == axis, moved, 0.0)
    own_ext = grown[0:4]
    tiles = cells // 128

    def put_sep(number, value):
        for tile in range(tiles):
            sep_ref[tile, pl.ds(number, 64, stride=16), :] = value[:, tile * 128 : tile * 128 + 128]

    def get_sep(window):
        return jnp.concatenate([sep_ref[tile, window, :] for tile in range(tiles)], axis=1)

    for number, (ox, oy, oz) in enumerate(offsets):
        distance = (ox * ext + oy) * ext + oz
        put_sep(number, pltpu.roll(grown, cells - distance, 1) - grown)
    for number in range(half, 16):
        put_sep(number, grown)

    picks_low = picks.astype(bf16)
    row16 = iota((16, cells), 0)

    def basis_of(domain):
        first = pl.multiple_of(domain * 64, 64)
        sx, sy, sz, codes = [get_sep(pl.ds(first + 16 * part, 16)) for part in range(4)]
        square = sx * sx + sy * sy + sz * sz
        near = jnp.minimum(jnp.sqrt(square), cutoff)
        base = jnp.maximum(1.0 - square * (1.0 / (cutoff * cutoff)), 0.0)
        value = jnp.exp(-gamma * jnp.minimum(square, cutoff * cutoff)) * base * base
        ratio = jnp.exp((2.0 * gamma * step) * near)
        out = []
        for number in range(NBASIS):
            hit = jnp.where(codes == number + 1.0, 1.0, 0.0)
            out.append(jnp.where(row16 == half, hit, value))
            value = value * ratio
        return jnp.concatenate(out, axis=0).astype(bf16)

    def basis_step(plane, carry):
        both = jnp.concatenate([basis_of(2 * plane), basis_of(2 * plane + 1)], axis=0)
        picked = dot(picks_low, both, nt)
        for tile in range(2):
            basis_ref[tile, pl.ds(plane, slots, stride=planes), :] = picked[
                :, tile * 128 : tile * 128 + 128
            ]
        return carry

    lax.fori_loop(0, planes, basis_step, 0)

    def wave_step(plane, carry):
        for part in range(2):
            for tile in range(2):
                lanes = slice(tile * 128, tile * 128 + 128)
                block = sites_ref[pl.ds(pl.multiple_of(plane * 8, 8), 8), lanes]
                coords_here = [block[part * 4 + axis : part * 4 + axis + 1] for axis in range(3)]
                coords_here[0] = coords_here[0] + (plane // 2).astype(f32) * domain_width
                coords_here[1] = coords_here[1] + (plane % 2).astype(f32) * domain_width
                coords_here[2] = coords_here[2] + part * domain_width
                start = pl.multiple_of(plane * pad + tile * 128, 128)

                def store(index, value):
                    waves_ref[part, index * 16 : index * 16 + 16, pl.ds(start, 128)] = value

                wave_tile(coords_here, store)
        return carry

    lax.fori_loop(0, planes, wave_step, 0)
    for tile in range(cells // 128):
        lanes = slice(tile * 128, tile * 128 + 128)

        def store(index, value):
            ring_ref[index * 16 : index * 16 + 16, lanes] = value

        wave_tile([own_ext[axis : axis + 1, lanes] for axis in range(3)], store)

    basis_low = jnp.concatenate([basis_ref[0], basis_ref[1]], axis=1).astype(bf16)
    for number in range(half):
        filters_ref[number] = dot(basis_low, radial_ref[number])
    start_values = dot(basis_low, embed_ref[...])
    rows_ref = basis_ref.at[0]
    live_ref = basis_ref.at[1]
    live_ref[...] = start_values[:, 256:384]
    set_inner(zero_ref, start_values[:, :128] + start_values[:, 128:256])
    fill_ghosts(zero_ref)
    convolve(filters_ref, 0, zero_ref, sum_ref)
    first_rows = inner_rows(zero_ref) + live_ref[...] * dot_split(
        inner_rows(sum_ref), mix_ref[0], mix_ref[1]
    )
    set_inner(one_ref, first_rows)
    rows_ref[...] = first_rows
    fill_ghosts(one_ref)

    def pack_rows():
        for plane in range(planes):
            value = rows_ref[pl.ds(plane, slots, stride=planes), :]
            packed_ref[plane * pad : plane * pad + pad, :] = jnp.concatenate(
                [value, jnp.zeros((pad - slots, 128), f32)], axis=0
            ).astype(bf16)

    def structure():
        low = dot(waves_ref[0], packed_ref[...])
        high = dot(waves_ref[1], packed_ref[...])
        return (low[:, :chan] + high[:, chan:]) * gain_ref[...]

    pack_rows()
    own_ref[...] = jnp.zeros(own_ref.shape, f32)
    own_ref[0, 0:slots] = rows_ref[pl.ds(0, slots, stride=planes), :]
    filtered = structure()
    filtered_rows = filtered.T.astype(bf16)
    long_rows = jnp.concatenate(
        [dot(filtered_rows, waves_ref[0]), dot(filtered_rows, waves_ref[1])], axis=0
    )
    for plane in range(planes):
        turned = long_rows[:, plane * pad : plane * pad + pad].T
        rows_ref[pl.ds(plane, slots, stride=planes), :] = turned[:slots]
    convolve(filters_ref, 1, one_ref, sum_ref)
    joined = jnp.concatenate([inner_rows(one_ref) + rows_ref[...], inner_rows(sum_ref)], axis=1)
    act = dot_split(joined, act_ref[0], act_ref[1]) + bias_ref[...]
    sig = 1.0 / (1.0 + jnp.exp(-act))
    weighted = live_ref[...] * energy_ref[...] * sig
    rows_ref[...] = weighted * act
    own_energy = rows_ref[pl.ds(0, slots, stride=planes), :]
    first_half = jnp.where(iota((8, 128), 1) < chan, 1.0, 0.0)
    site_energy = dot(first_half, own_energy, nt, highest)[0:1]
    grads = dot_split(weighted * (1.0 + act * (1.0 - sig)), grad_ref[0], grad_ref[1])
    rows_ref[...] = grads[:, :128]
    set_inner(two_ref, grads[:, 128:])
    fill_ghosts(two_ref)
    pack_rows()
    own_ref[1, 0:slots] = rows_ref[pl.ds(0, slots, stride=planes), :]
    back = structure()
    back_rows = back.T.astype(bf16)
    flat = (cells * planes, 128)
    own_cells = pl.ds(0, cells, stride=planes)
    one_cells = one_ref.reshape(flat)[own_cells, :][:, :chan]
    two_cells = two_ref.reshape(flat)[own_cells, :][:, :chan]
    zero_cells = zero_ref.reshape(flat)[own_cells, :][:, :chan]
    convolve(filters_ref, 1, two_ref, sum_ref)
    set_inner(sum_ref, rows_ref[...] + live_ref[...] * inner_rows(sum_ref))
    fill_ghosts(sum_ref)
    sum_cells = sum_ref.reshape(flat)[own_cells, :][:, :chan]
    live_cells = jnp.where(own_ext[3:4] > 0, 1.0, 0.0)
    ring_long = (dot(back_rows, ring_ref[...]) * live_cells).T
    grad_cells = dot_split(sum_cells + ring_long, back_ref[0], back_ref[1])

    def crossed(value):
        value = value.reshape(waves // 8, 2, 8, chan)
        value = jnp.concatenate([value[:, 1:2], -value[:, 0:1]], axis=1).reshape(table, chan)
        return jnp.concatenate([value, jnp.zeros((table, chan), f32)], axis=1).astype(bf16)

    response = dot(crossed(filtered), own_ref[1].astype(bf16), nt) + dot(
        crossed(back), own_ref[0].astype(bf16), nt
    )
    turning_high, turning_low = split(waves_ref[0, :, 0:pad].astype(f32) * response)
    spot = iota((8, table), 1)
    wave = spot // 16 * 8 + spot % 8

    def signed(index):
        return jnp.where(index % 2 == 1, (index + 1) // 2, -(index // 2))

    row = iota((8, table), 0)
    number = jnp.where(
        row == 0,
        wave % 8 + 1,
        jnp.where(row == 1, signed(wave // 72), jnp.where(row == 2, signed(wave // 8 % 9), 0)),
    )
    number = number.astype(f32).astype(bf16)
    scale_row = iota((8, 1), 0)
    scales = jnp.where(
        scale_row == 0,
        two_pi / (grid_dims[0] * domain_width),
        two_pi / (grid_dims[1] * domain_width),
    )
    long_force = (dot(number, turning_high) + dot(number, turning_low))[:, :slots] * scales

    left = [
        jnp.concatenate([two_cells, one_cells], axis=1),
        jnp.concatenate([grad_cells, zero_cells], axis=1),
    ]
    right = jnp.concatenate(
        [
            jnp.concatenate([one_cells, two_cells], axis=1),
            jnp.concatenate([zero_cells, grad_cells], axis=1),
        ],
        axis=1,
    )
    shift_ref[0:cells] = right
    shift_ref[cells:] = jnp.zeros((shift_ref.shape[0] - cells, 256), f32)
    left = jnp.concatenate(left, axis=1)
    centre = step * iota((8, cells), 0).astype(f32)
    sep = [get_sep(slice(16 * part, 16 * part + 16)) for part in range(3)]
    square = sep[0] * sep[0] + sep[1] * sep[1] + sep[2] * sep[2]
    length = jnp.sqrt(square)
    inverse = 1.0 / length
    base = jnp.maximum(1.0 - square * (1.0 / (cutoff * cutoff)), 0.0)
    inward = length * base * (-4.0 / (cutoff * cutoff))
    outward = (-2.0 * gamma) * base * base
    totals = [jnp.zeros((1, cells), f32)] * 3
    for number, (ox, oy, oz) in enumerate(offsets):
        distance = (ox * ext + oy) * ext + oz
        products = (left * shift_ref[distance : distance + cells]).astype(bf16)
        shares = dot(pair_ref[...], products, nt)
        shares = shares[:8] + shares[8:]
        row = slice(number, number + 1)
        gap = length[row] - centre
        slope = jnp.exp(-gamma * gap * gap) * (inward[row] + gap * outward[row])
        strength = jnp.sum(slope * shares, axis=0, keepdims=True) * inverse[row]
        for part in range(3):
            force = sep[part][row] * strength
            totals[part] = totals[part] + pltpu.roll(force, distance, 1) - force
    total = jnp.concatenate(totals + [jnp.zeros((5, cells), f32)], axis=0)
    site_total = dot(total, picks, nt, highest)
    lines = jnp.concatenate([-(site_total[0:3] + long_force[0:3]), site_energy], axis=0)
    lines = jnp.concatenate([lines, jnp.zeros((4, slots), f32)], axis=0)
    hot = (iota((slots, slots), 0) == site_of(pos_ref[...])).astype(f32)
    out_ref[...] = dot(lines, hot, nn, highest)


def kernel_params():
    return pltpu.CompilerParams(vmem_limit_bytes=63 * 1024 * 1024)


def whole_box(
    species,
    counts,
    positions,
    ghost_rows,
    neighbours,
    kvec,
    embed,
    radial_one,
    radial_two,
    mix_one,
    mix_two,
    lr_filter,
    read_weight,
    read_bias,
    energy_weight,
):
    axes = ("gx", "gy", "gz")
    coords = positions.reshape(3, slots)
    vmem = pl.BlockSpec(memory_space=pltpu.VMEM)
    smem = pl.BlockSpec(memory_space=pltpu.SMEM)
    placed = pl.pallas_call(
        place_kernel,
        out_shape=jax.ShapeDtypeStruct((4, slots), f32),
        in_specs=[smem, vmem, vmem],
        out_specs=vmem,
    )(counts.reshape(1), coords, species.reshape(1, slots))
    shared = lax.all_to_all(
        jnp.broadcast_to(placed[None], (domains, 4, slots)), axes, 0, 0, tiled=True
    )
    prepared = pl.pallas_call(
        weights_kernel,
        out_shape=(
            jax.ShapeDtypeStruct((table, chan), f32),
            jax.ShapeDtypeStruct((half, pad, pad), bf16),
            jax.ShapeDtypeStruct((pad, 384), bf16),
            jax.ShapeDtypeStruct((2, 128, 128), bf16),
            jax.ShapeDtypeStruct((2, 256, 128), bf16),
            jax.ShapeDtypeStruct((2, 128, 256), bf16),
            jax.ShapeDtypeStruct((2, chan, chan), bf16),
            jax.ShapeDtypeStruct((16, 256), bf16),
        ),
        in_specs=[vmem] * 8,
        out_specs=(vmem,) * 8,
        compiler_params=kernel_params(),
    )(kvec, lr_filter, embed, radial_one, radial_two, mix_one, mix_two, read_weight)
    place = jnp.stack([lax.axis_index(axis) for axis in axes]).astype(jnp.int32)
    result = box_call(
        place, shared, coords, prepared, read_bias.reshape(1, chan), energy_weight.reshape(1, chan)
    )
    return (result[3].reshape(1, 1, 1, slots), result[:3].reshape(1, 1, 1, 3, slots))


def box_call(place, shared, coords, prepared, bias, energy, interpret=False):
    vmem = pl.BlockSpec(memory_space=pltpu.VMEM)
    smem = pl.BlockSpec(memory_space=pltpu.SMEM)
    grid_shape = (ext, ext, ext, planes, 128)
    return pl.pallas_call(
        box_kernel,
        out_shape=jax.ShapeDtypeStruct((8, slots), f32),
        in_specs=[smem] + [vmem] * 12,
        out_specs=vmem,
        scratch_shapes=[
            pltpu.VMEM((cells // 128, 64 * 16, 128), f32),
            pltpu.VMEM((64, pad), f32),
            pltpu.VMEM((2, rows_all, 128), f32),
            pltpu.VMEM((half, rows_all, pad), f32),
            pltpu.VMEM((2, table, planes * pad), bf16),
            pltpu.VMEM((table, cells), bf16),
            pltpu.VMEM(grid_shape, f32),
            pltpu.VMEM(grid_shape, f32),
            pltpu.VMEM(grid_shape, f32),
            pltpu.VMEM(grid_shape, f32),
            pltpu.VMEM((planes * pad, 128), bf16),
            pltpu.VMEM((cells + 80, 256), f32),
            pltpu.VMEM((2, pad, 128), f32),
        ],
        compiler_params=kernel_params(),
        interpret=interpret,
    )(
        place,
        shared,
        coords,
        *prepared,
        jnp.concatenate([bias, bias], axis=1),
        jnp.concatenate([energy, energy], axis=1),
    )


def solution(mesh):
    in_specs = (
        P(("group", "gx"), "gy", "gz", None),
        P(("group", "gx"), "gy", "gz"),
        P(("group", "gx"), "gy", "gz", None, None),
        P(("group", "gx"), "gy", "gz", None),
        P(("group", "gx"), "gy", "gz", None, None),
        P(),
        P(),
        P(),
        P(),
        P(),
        P(),
        P(),
        P(),
        P(),
        P(),
    )
    out_specs = (P(("group", "gx"), "gy", "gz", None), P(("group", "gx"), "gy", "gz", None, None))
    sizes = tuple(mesh.shape[axis] for axis in ("gx", "gy", "gz"))
    plan = whole_box if sizes == grid_dims else local
    return jax.shard_map(plan, mesh=mesh, in_specs=in_specs, out_specs=out_specs, check_vma=False)
```

profile of v0, /device:TPU:0, one launch (start us, length us, event | category | flops | bytes accessed | tf_op | source)
XLA Modules:
  0.0 65.8 jit_solution(6009499261241757595)
XLA Ops:
  1.3 1.3 %copy.18 = f32[1,1,1,3,216]{4,3,2,1,0:T(4,128)} copy(f32[1,1,1,3,216]{4,2,3,1,0:T(1,128)} %param.17) | data formatting | bytes 5184
  2.5 1.6 %shard_map.140 = f32[4,216]{1,0:T(4,128)} custom-call(s32[1]{0:T(128)} %bitcast.14.count_ref, f32[3,216]{1,0:T(4,128)} %bitcast.15, s32[1,216]{1,0:T(1,128)} %bitcast.17), custom_call_target="tpu_custom_call" | custom-call | tf_op jit(solution)/shard_map/pallas_call | solution.py:1108
  4.1 1.3 %broadcast_in_dim.2 = f32[16,4,216]{2,1,0:T(4,128)} broadcast(f32[4,216]{1,0:T(4,128)} %shard_map.140), dimensions={1,2} | broadcast | bytes 58752 | tf_op jit(solution)/shard_map/broadcast_in_dim | solution.py:1115
  5.4 7.4 %all-to-all-start = ((f32[16,4,216]{2,1,0:T(4,128)}), f32[16,4,216]{2,1,0:T(4,128)S(1)}, u32[]{:S(2)}, u32[]{:S(2)}) async-start(f32[16,4,216]{2,1,0:T(4,128)} %broadcast_in_dim.2), calls=%async_computation | async-start | bytes 131072 | tf_op jit(solution)/shard_map/all_to_all | solution.py:1114
  12.8 1.3 %pad_maximum_fusion = (f32[1,128]{1,0:T(1,128)}, f32[1,128]{1,0:T(1,128)}) fusion(f32[1,64]{1,0:T(1,128)} %bitcast.18, f32[1,64]{1,0:T(1,128)} %bitcast.19), kind=kLoop, calls=%fused_computation.4 | loop fusion | flops 256 | bytes 1536 | tf_op jit(solution)/shard_map/concatenate | solution.py:1171
  14.1 4.7 %shard_map.141 = (f32[1296,64]{1,0:T(8,128)}, bf16[13,256,256]{2,1,0:T(8,128)(2,1)}, bf16[256,384]{1,0:T(8,128)(2,1)}, bf16[2,128,128]{2,1,0:T(8,128)(2,1)}, bf1...) custom-call(s32[3,4096]{1,0:T(4,128)} %kvec_ref.1, ...), custom_call_target="tpu_custom_call" | custom-call | tf_op jit(solution)/shard_map/pallas_call | solution.py:1117
  18.9 0.7 %pad_add_fusion.place_ref = s32[3]{0:T(128)} fusion(s32[1]{0:T(128)} %bitcast.2, s32[1]{0:T(128)} %bitcast.1, s32[1]{0:T(128)} %bitcast), kind=kLoop, calls=%fused_computation.3 | loop fusion | flops 6 | bytes 24 | tf_op jit(solution)/shard_map/stack | solution.py:1133
  19.5 0.2 all-to-all-done.all_ref
  19.7 0.0 copy-start
  19.7 0.6 copy-done
  20.3 42.9 %shard_map.142 = f32[8,216]{1,0:T(8,128)} custom-call(s32[3]{0:T(128)} %pad_add_fusion.place_ref, f32[16,4,216]{2,1,0:T(4,128)} %copy-done, f32[3,216]{1,0:T(4,128)} %bitcast.16, f32[1296,64]{1,0:T(8,128)} %get-tuple-element.10.gain_ref, bf16[13,256,256]{2,1,0:T(8,128)(2,1)} %get-tuple-element.11.radial_ref, bf16[256,384]{1,0:T(8,128)(2,1)} %get-tuple-element.12.embed_ref, ...), custom_call_target="tpu_custom_call" | custom-call | tf_op jit(solution)/shard_map/pallas_call | solution.py:1144
  63.2 1.3 %slice_bitcast_fusion.1 = f32[1,1,1,216]{3,2,1,0:T(1,128)} fusion(f32[8,216]{1,0:T(8,128)} %shard_map.142), kind=kLoop, calls=%fused_computation.2 | loop fusion | bytes 1728 | tf_op jit(solution)/shard_map/reshape;squeeze | solution.py:1137
  64.5 0.7 %slice_bitcast_fusion = f32[1,1,1,3,216]{4,3,2,1,0:T(4,128)S(1)} fusion(f32[8,216]{1,0:T(8,128)} %shard_map.142), kind=kLoop, calls=%fused_computation | loop fusion | bytes 5184 | tf_op jit(solution)/shard_map/reshape | solution.py:1137
  65.2 0.6 copy.15
Async XLA Ops:
  5.4 14.3 %all-to-all-start = ((f32[16,4,216]{2,1,0:T(4,128)}), f32[16,4,216]{2,1,0:T(4,128)S(1)}, u32[]{:S(2)}, u32[]{:S(2)}) async-start(f32[16,4,216]{2,1,0:T(4,128)} %broadcast_in_dim.2), calls=%async_computation | async-start | bytes 131072 | tf_op jit(solution)/shard_map/all_to_all | solution.py:1114
  19.7 0.6 copy-start
where the time goes:
time: 66.2 us; the launch traced here: 65.8 us
  Pallas kernels  49.2 us (74%)
  starting transfers between devices  7.36 us (11%)
  local copies, waits for them, and re-layouts  5.73 us (9%)
  other arithmetic  2 us (3%)
  between operations  1.3 us (2%)
    pallas_call x1, Pallas kernels, box_call(): pl.pallas_call(box_kernel, out_shape=jax.ShapeDtypeStruct((8, slots), f32...  42.9 us
    all_to_all x1, starting transfers between devices, whole_box(): lax.all_to_all(jnp.broadcast_to(placed[None], (domains, 4, slots)), axes,...  7.36 us
    pallas_call x1, Pallas kernels, whole_box(): pl.pallas_call(weights_kernel, out_shape=(jax.ShapeDtypeStruct((table, ch...  4.73 us
    unnamed x4, local copies, waits for them, and re-layouts  2.48 us
    pallas_call x1, Pallas kernels, whole_box(): pl.pallas_call(place_kernel, out_shape=jax.ShapeDtypeStruct((4, slots), f...  1.57 us
    concatenate x1, other arithmetic, box_call(): jnp.concatenate([bias, bias], axis=1)  1.34 us
  transfers between devices with their start and end apart: 1, of which 1 were waited for; matrix products, arithmetic and copies ran while one was open for 3% of the time, Pallas kernels for 7%

commit v1 on v0

--- a/solution.py
+++ b/solution.py
@@ -516,6 +516,7 @@
 slots = SIDE**3
 ext = SIDE + 2
 cells = ext**3
+inner_lanes = SIDE * ext * ext
 chan = 64
 grid_dims = (4, 2, 2)
 domains = 16
@@ -546,6 +547,20 @@
     return dot(left_high, high) + dot(left_low, high) + dot(left_high, low)
 
 
+def exact(left, hot, dims=nn):
+    high = left.astype(bf16).astype(f32)
+    rest = left - high
+    middle = rest.astype(bf16).astype(f32)
+    count = left.shape[0]
+    stacked = jnp.concatenate([high, middle, rest - middle], axis=0).astype(bf16)
+    parts = dot(stacked, hot, dims)
+    return parts[:count] + parts[count : 2 * count] + parts[2 * count :]
+
+
+def coords_of(ref):
+    return jnp.concatenate([ref[0, 0, axis] for axis in range(3)], axis=0)
+
+
 def site_of(coords):
     where = (coords * (1.0 / spacing)).astype(jnp.int32)
     return (where[0:1] * SIDE + where[1:2]) * SIDE + where[2:3]
@@ -556,12 +571,14 @@
 
 
 def place_kernel(count_ref, pos_ref, species_ref, out_ref):
-    coords = pos_ref[...]
-    live = iota((1, slots), 1) < count_ref[0]
-    code = jnp.where(live, species_ref[...] + 1, 0).astype(f32)
-    data = jnp.concatenate([coords, code], axis=0)
-    hot = (iota((slots, slots), 0) == site_of(coords)).astype(f32)
-    out_ref[...] = dot(data, hot, nt, highest)
+    coords = coords_of(pos_ref)
+    live = iota((1, slots), 1) < count_ref[0, 0, 0]
+    code = jnp.where(live, species_ref[0, 0] + 1, 0).astype(f32)
+    data = jnp.concatenate([coords, code, jnp.zeros((4, slots), f32)], axis=0)
+    hot = (iota((slots, slots), 0) == site_of(coords)).astype(f32).astype(bf16)
+    placed = exact(data, hot, nt)[0:4]
+    for number in range(domains):
+        out_ref[number] = placed
 
 
 def twice(block):
@@ -580,6 +597,8 @@
     mix_one_ref,
     mix_two_ref,
     read_ref,
+    bias_ref,
+    energy_ref,
     gain_ref,
     radial_ref,
     embed_out,
@@ -588,6 +607,7 @@
     grad_ref,
     back_ref,
     pair_ref,
+    lines_ref,
 ):
     pair_scale = 1.0 / math.sqrt(NEIGH)
     wave_scale = 1.0 / math.sqrt(KVEC * slots * domains)
@@ -636,6 +656,10 @@
         ref[0] = value_high
         ref[1] = value_low
 
+    bias = bias_ref[...]
+    energy = energy_ref[...]
+    lines_ref[0:1] = jnp.concatenate([bias, bias], axis=1)
+    lines_ref[1:2] = jnp.concatenate([energy, energy], axis=1)
     mix_two = mix_two_ref[...]
     read = read_ref[...]
     both = dot(mix_two, read, nn, highest) * pair_scale
@@ -644,8 +668,9 @@
     put(grad_ref, jnp.concatenate([twice(read.T), twice(both.T)], axis=1))
     put(back_ref, mix_one_ref[...].T * pair_scale)
     pairs = jnp.concatenate([two_ref[...], two_ref[...], one_ref[...], one_ref[...]], axis=1)
-    pairs_high = pairs.astype(bf16).astype(f32)
-    pair_ref[...] = jnp.concatenate([pairs_high, pairs - pairs_high], axis=0).astype(bf16)
+    pairs = jnp.broadcast_to(pairs[:, None, :], (NBASIS, 16, 256)).reshape(128, 256).T
+    for offset in range(half):
+        pair_ref[offset] = jnp.where(columns[:, :128] % 16 == offset, pairs, 0.0).astype(bf16)
 
 
 def turn(fraction):
@@ -762,14 +787,14 @@
     ref[inner, inner, inner] = value.reshape(SIDE, SIDE, SIDE, planes, 128)
 
 
-def convolve(filters, layer, source, target):
+def convolve(filters, layer, source, target, beside=None):
     target[...] = jnp.zeros(target.shape, f32)
     lanes = slice(layer * 128, layer * 128 + 128)
     groups = {}
     for number, (ox, oy, oz) in enumerate(offsets):
         groups.setdefault((ox, oy), []).append((number, oz))
 
-    def body(line, carry):
+    def one_line(line):
         x = line // SIDE
         y = line % SIDE
         own = [source[x + 1, y + 1, z + 1] for z in range(SIDE)]
@@ -790,9 +815,15 @@
                     target[x + 1 + ox, y + 1 + oy, z] = target[x + 1 + ox, y + 1 + oy, z] + sums[z]
         for z in range(SIDE):
             target[x + 1, y + 1, z + 1] = target[x + 1, y + 1, z + 1] + own_sum[z]
+
+    def body(number, carry):
+        if beside is not None:
+            beside(number)
+        for part in range(3):
+            one_line(number * 3 + part)
         return carry
 
-    lax.fori_loop(0, SIDE * SIDE, body, 0)
+    lax.fori_loop(0, SIDE * SIDE // 3, body, 0)
     fold_ghosts(target)
 
 
@@ -808,9 +839,9 @@
     grad_ref,
     back_ref,
     pair_ref,
-    bias_ref,
-    energy_ref,
-    out_ref,
+    lines_ref,
+    energy_out,
+    force_out,
     sep_ref,
     sites_ref,
     basis_ref,
@@ -819,34 +850,43 @@
     ring_ref,
     zero_ref,
     one_ref,
-    two_ref,
     sum_ref,
     packed_ref,
-    shift_ref,
     own_ref,
+    flat_ref,
+    low_ref,
+    parts_ref,
+    saved_ref,
 ):
     home = [place_ref[axis] for axis in range(3)]
     sites_ref[...] = jnp.zeros((4 * domains, pad), f32)
+    domain_width = SIDE * spacing
+    offset_row = iota((4, slots), 0)
     for number in range(domains):
         spot = [
             lax.rem(home[axis] + part, grid_dims[axis])
             for axis, part in enumerate((number // 4, number // 2 % 2, number % 2))
         ]
-        sites_ref[number * 4 : number * 4 + 4, 0:slots] = all_ref[
-            (spot[0] * 2 + spot[1]) * 2 + spot[2]
-        ]
+        block = all_ref[(spot[0] * 2 + spot[1]) * 2 + spot[2]]
+        sites_ref[number * 4 : number * 4 + 4, 0:slots] = block
+        shifts = [part * domain_width for part in (number // 4, number // 2 % 2, number % 2)]
+        moved = jnp.where(
+            offset_row == 0, shifts[0], jnp.where(offset_row == 1, shifts[1], shifts[2])
+        )
+        start = (number % 2 * planes + number // 2) * slots
+        flat_ref[0:4, start : start + slots] = block + moved
     sites = sites_ref[:, 0:slots]
 
     lane = iota((1, cells), 1)
-    coords = [lane // (ext * ext), lane // ext % ext, lane % ext]
+    coords = [(lane // (ext * ext) + 1) % ext, lane // ext % ext, lane % ext]
     wrapped = [(value + SIDE - 1) % SIDE for value in coords]
     wrapped_site = (wrapped[0] * SIDE + wrapped[1]) * SIDE + wrapped[2]
     inside = coords[0] >= 0
     for value in coords:
         inside = inside & (value > 0) & (value < ext - 1)
     hot_all = iota((slots, cells), 0) == wrapped_site
-    grown = dot(sites, hot_all.astype(f32), nn, highest)
-    picks = (hot_all & inside).astype(f32)
+    grown = exact(sites, hot_all.astype(f32).astype(bf16))
+    picks = (hot_all & inside)[:, :inner_lanes].astype(f32).astype(bf16)
 
     back16 = jnp.concatenate([grown[48:], grown[:48]], axis=0)
     ahead16 = jnp.concatenate([grown[16:], grown[:16]], axis=0)
@@ -858,7 +898,6 @@
     swapped = pltpu.roll(grown.reshape(8, 8, cells), 4, 1).reshape(64, cells)
     grown = jnp.where((coords[2] == 0) | (coords[2] == ext - 1), swapped, grown)
     component = iota((64, cells), 0) % 4
-    domain_width = SIDE * spacing
     for axis in range(3):
         moved = jnp.where(
             coords[axis] == 0,
@@ -873,8 +912,8 @@
         for tile in range(tiles):
             sep_ref[tile, pl.ds(number, 64, stride=16), :] = value[:, tile * 128 : tile * 128 + 128]
 
-    def get_sep(window):
-        return jnp.concatenate([sep_ref[tile, window, :] for tile in range(tiles)], axis=1)
+    def get_sep(window, count=tiles):
+        return jnp.concatenate([sep_ref[tile, window, :] for tile in range(count)], axis=1)
 
     for number, (ox, oy, oz) in enumerate(offsets):
         distance = (ox * ext + oy) * ext + oz
@@ -882,12 +921,11 @@
     for number in range(half, 16):
         put_sep(number, grown)
 
-    picks_low = picks.astype(bf16)
-    row16 = iota((16, cells), 0)
+    row16 = iota((16, inner_lanes), 0)
 
     def basis_of(domain):
         first = pl.multiple_of(domain * 64, 64)
-        sx, sy, sz, codes = [get_sep(pl.ds(first + 16 * part, 16)) for part in range(4)]
+        sx, sy, sz, codes = [get_sep(pl.ds(first + 16 * part, 16), inner_lanes // 128) for part in range(4)]
         square = sx * sx + sy * sy + sz * sz
         near = jnp.minimum(jnp.sqrt(square), cutoff)
         base = jnp.maximum(1.0 - square * (1.0 / (cutoff * cutoff)), 0.0)
@@ -902,7 +940,7 @@
 
     def basis_step(plane, carry):
         both = jnp.concatenate([basis_of(2 * plane), basis_of(2 * plane + 1)], axis=0)
-        picked = dot(picks_low, both, nt)
+        picked = dot(picks, both, nt)
         for tile in range(2):
             basis_ref[tile, pl.ds(plane, slots, stride=planes), :] = picked[
                 :, tile * 128 : tile * 128 + 128
@@ -911,24 +949,25 @@
 
     lax.fori_loop(0, planes, basis_step, 0)
 
-    def wave_step(plane, carry):
+    basis_low = jnp.concatenate([basis_ref[0], basis_ref[1]], axis=1).astype(bf16)
+    low_ref[...] = basis_low
+
+    def flat_tile(start):
+        block = flat_ref[:, pl.ds(start, 128)]
+
+        def store(index, value):
+            waves_ref[index * 16 : index * 16 + 16, pl.ds(start, 128)] = value
+
+        wave_tile([block[axis : axis + 1] for axis in range(3)], store)
+
+    def wave_step(number, carry):
+        filters_ref[number] = dot(low_ref[...], radial_ref[number])
         for part in range(2):
-            for tile in range(2):
-                lanes = slice(tile * 128, tile * 128 + 128)
-                block = sites_ref[pl.ds(pl.multiple_of(plane * 8, 8), 8), lanes]
-                coords_here = [block[part * 4 + axis : part * 4 + axis + 1] for axis in range(3)]
-                coords_here[0] = coords_here[0] + (plane // 2).astype(f32) * domain_width
-                coords_here[1] = coords_here[1] + (plane % 2).astype(f32) * domain_width
-                coords_here[2] = coords_here[2] + part * domain_width
-                start = pl.multiple_of(plane * pad + tile * 128, 128)
-
-                def store(index, value):
-                    waves_ref[part, index * 16 : index * 16 + 16, pl.ds(start, 128)] = value
-
-                wave_tile(coords_here, store)
+            flat_tile(pl.multiple_of(number * 256 + part * 128, 128))
         return carry
 
-    lax.fori_loop(0, planes, wave_step, 0)
+    lax.fori_loop(0, half, wave_step, 0)
+    flat_tile(half * 256)
     for tile in range(cells // 128):
         lanes = slice(tile * 128, tile * 128 + 128)
 
@@ -937,9 +976,6 @@
 
         wave_tile([own_ext[axis : axis + 1, lanes] for axis in range(3)], store)
 
-    basis_low = jnp.concatenate([basis_ref[0], basis_ref[1]], axis=1).astype(bf16)
-    for number in range(half):
-        filters_ref[number] = dot(basis_low, radial_ref[number])
     start_values = dot(basis_low, embed_ref[...])
     rows_ref = basis_ref.at[0]
     live_ref = basis_ref.at[1]
@@ -947,62 +983,75 @@
     set_inner(zero_ref, start_values[:, :128] + start_values[:, 128:256])
     fill_ghosts(zero_ref)
     convolve(filters_ref, 0, zero_ref, sum_ref)
+    flat = (cells * planes, 128)
+    own_cells = pl.ds(0, cells, stride=planes)
+
+    def cells_of(ref):
+        value = ref.reshape(flat)[own_cells, :]
+        return jnp.concatenate([value[ext * ext :], value[: ext * ext]], axis=0)[:, :chan]
+
+    saved_ref[0] = cells_of(zero_ref)
     first_rows = inner_rows(zero_ref) + live_ref[...] * dot_split(
         inner_rows(sum_ref), mix_ref[0], mix_ref[1]
     )
     set_inner(one_ref, first_rows)
     rows_ref[...] = first_rows
     fill_ghosts(one_ref)
+    saved_ref[1] = cells_of(one_ref)
+    two_ref = zero_ref
 
     def pack_rows():
         for plane in range(planes):
             value = rows_ref[pl.ds(plane, slots, stride=planes), :]
-            packed_ref[plane * pad : plane * pad + pad, :] = jnp.concatenate(
-                [value, jnp.zeros((pad - slots, 128), f32)], axis=0
-            ).astype(bf16)
+            packed_ref[plane * slots : plane * slots + slots] = value
+            packed_ref[rows_all + plane * slots : rows_all + plane * slots + slots] = pltpu.roll(
+                value, chan, 1
+            )
+        tail = 12 * pad
+        parts_ref[...] = dot(waves_ref[:, tail:], packed_ref[tail:].astype(bf16))
+
+    def structure_step(number):
+        start = pl.multiple_of(number * pad, pad)
+        parts_ref[...] = parts_ref[...] + dot(
+            waves_ref[:, pl.ds(start, pad)], packed_ref[pl.ds(start, pad), :].astype(bf16)
+        )
 
     def structure():
-        low = dot(waves_ref[0], packed_ref[...])
-        high = dot(waves_ref[1], packed_ref[...])
-        return (low[:, :chan] + high[:, chan:]) * gain_ref[...]
+        return parts_ref[:, :chan] * gain_ref[...]
 
     pack_rows()
     own_ref[...] = jnp.zeros(own_ref.shape, f32)
     own_ref[0, 0:slots] = rows_ref[pl.ds(0, slots, stride=planes), :]
+    convolve(filters_ref, 1, one_ref, sum_ref, structure_step)
     filtered = structure()
-    filtered_rows = filtered.T.astype(bf16)
-    long_rows = jnp.concatenate(
-        [dot(filtered_rows, waves_ref[0]), dot(filtered_rows, waves_ref[1])], axis=0
-    )
+    long_rows = dot(filtered.T.astype(bf16), waves_ref[...]).T
     for plane in range(planes):
-        turned = long_rows[:, plane * pad : plane * pad + pad].T
-        rows_ref[pl.ds(plane, slots, stride=planes), :] = turned[:slots]
-    convolve(filters_ref, 1, one_ref, sum_ref)
+        first = long_rows[plane * slots : plane * slots + slots]
+        second = long_rows[rows_all + plane * slots : rows_all + plane * slots + slots]
+        rows_ref[pl.ds(plane, slots, stride=planes), :] = jnp.concatenate([first, second], axis=1)
     joined = jnp.concatenate([inner_rows(one_ref) + rows_ref[...], inner_rows(sum_ref)], axis=1)
-    act = dot_split(joined, act_ref[0], act_ref[1]) + bias_ref[...]
+    act = dot_split(joined, act_ref[0], act_ref[1]) + lines_ref[0:1]
     sig = 1.0 / (1.0 + jnp.exp(-act))
-    weighted = live_ref[...] * energy_ref[...] * sig
+    weighted = live_ref[...] * lines_ref[1:2] * sig
     rows_ref[...] = weighted * act
     own_energy = rows_ref[pl.ds(0, slots, stride=planes), :]
     first_half = jnp.where(iota((8, 128), 1) < chan, 1.0, 0.0)
-    site_energy = dot(first_half, own_energy, nt, highest)[0:1]
+    energy_high, energy_low = split(own_energy)
+    first_half = first_half.astype(bf16)
+    site_energy = (dot(first_half, energy_high, nt) + dot(first_half, energy_low, nt))[0:1]
     grads = dot_split(weighted * (1.0 + act * (1.0 - sig)), grad_ref[0], grad_ref[1])
     rows_ref[...] = grads[:, :128]
     set_inner(two_ref, grads[:, 128:])
     fill_ghosts(two_ref)
     pack_rows()
     own_ref[1, 0:slots] = rows_ref[pl.ds(0, slots, stride=planes), :]
+    two_cells = cells_of(two_ref)
+    convolve(filters_ref, 1, two_ref, sum_ref, structure_step)
     back = structure()
     back_rows = back.T.astype(bf16)
-    flat = (cells * planes, 128)
-    own_cells = pl.ds(0, cells, stride=planes)
-    one_cells = one_ref.reshape(flat)[own_cells, :][:, :chan]
-    two_cells = two_ref.reshape(flat)[own_cells, :][:, :chan]
-    zero_cells = zero_ref.reshape(flat)[own_cells, :][:, :chan]
-    convolve(filters_ref, 1, two_ref, sum_ref)
     set_inner(sum_ref, rows_ref[...] + live_ref[...] * inner_rows(sum_ref))
     fill_ghosts(sum_ref)
-    sum_cells = sum_ref.reshape(flat)[own_cells, :][:, :chan]
+    sum_cells = cells_of(sum_ref)
     live_cells = jnp.where(own_ext[3:4] > 0, 1.0, 0.0)
     ring_long = (dot(back_rows, ring_ref[...]) * live_cells).T
     grad_cells = dot_split(sum_cells + ring_long, back_ref[0], back_ref[1])
@@ -1015,7 +1064,7 @@
     response = dot(crossed(filtered), own_ref[1].astype(bf16), nt) + dot(
         crossed(back), own_ref[0].astype(bf16), nt
     )
-    turning_high, turning_low = split(waves_ref[0, :, 0:pad].astype(f32) * response)
+    turning_high, turning_low = split(waves_ref[:, 0:pad].astype(f32) * response)
     spot = iota((8, table), 1)
     wave = spot // 16 * 8 + spot % 8
 
@@ -1037,6 +1086,8 @@
     )
     long_force = (dot(number, turning_high) + dot(number, turning_low))[:, :slots] * scales
 
+    zero_cells = saved_ref[0]
+    one_cells = saved_ref[1]
     left = [
         jnp.concatenate([two_cells, one_cells], axis=1),
         jnp.concatenate([grad_cells, zero_cells], axis=1),
@@ -1048,36 +1099,47 @@
         ],
         axis=1,
     )
-    shift_ref[0:cells] = right
-    shift_ref[cells:] = jnp.zeros((shift_ref.shape[0] - cells, 256), f32)
     left = jnp.concatenate(left, axis=1)
-    centre = step * iota((8, cells), 0).astype(f32)
+    reach = ext * ext + 2 * ext
+    for shift in range(3):
+        moved = right if shift == 1 else pltpu.roll(right, (1 - shift) % cells, 0)
+        filters_ref[shift, 0:cells] = moved
+        filters_ref[shift, cells : cells + reach] = moved[:reach]
+    shares = jnp.zeros((cells, 128), f32)
+    for number, (ox, oy, oz) in enumerate(offsets):
+        distance = (ox * ext + oy) * ext
+        products = left * filters_ref[oz + 1, distance : distance + cells]
+        shares = shares + dot(products.astype(bf16), pair_ref[number])
+    shares = shares.T
     sep = [get_sep(slice(16 * part, 16 * part + 16)) for part in range(3)]
     square = sep[0] * sep[0] + sep[1] * sep[1] + sep[2] * sep[2]
     length = jnp.sqrt(square)
-    inverse = 1.0 / length
     base = jnp.maximum(1.0 - square * (1.0 / (cutoff * cutoff)), 0.0)
     inward = length * base * (-4.0 / (cutoff * cutoff))
     outward = (-2.0 * gamma) * base * base
-    totals = [jnp.zeros((1, cells), f32)] * 3
-    for number, (ox, oy, oz) in enumerate(offsets):
-        distance = (ox * ext + oy) * ext + oz
-        products = (left * shift_ref[distance : distance + cells]).astype(bf16)
-        shares = dot(pair_ref[...], products, nt)
-        shares = shares[:8] + shares[8:]
-        row = slice(number, number + 1)
-        gap = length[row] - centre
-        slope = jnp.exp(-gamma * gap * gap) * (inward[row] + gap * outward[row])
-        strength = jnp.sum(slope * shares, axis=0, keepdims=True) * inverse[row]
-        for part in range(3):
-            force = sep[part][row] * strength
-            totals[part] = totals[part] + pltpu.roll(force, distance, 1) - force
+    strength = jnp.zeros((16, cells), f32)
+    for number in range(NBASIS):
+        gap = length - step * number
+        slope = jnp.exp(-gamma * gap * gap) * (inward + gap * outward)
+        strength = strength + slope * shares[16 * number : 16 * number + 16]
+    strength = strength / length
+    totals = []
+    for part in range(3):
+        force = jnp.where(iota((16, cells), 0) < half, sep[part] * strength, 0.0)
+        total = -jnp.sum(force, axis=0, keepdims=True)
+        for number, (ox, oy, oz) in enumerate(offsets):
+            distance = (ox * ext + oy) * ext + oz
+            total = total + pltpu.roll(force[number : number + 1], distance, 1)
+        totals.append(total)
     total = jnp.concatenate(totals + [jnp.zeros((5, cells), f32)], axis=0)
-    site_total = dot(total, picks, nt, highest)
+    site_total = exact(total[:, :inner_lanes], picks, nt)
     lines = jnp.concatenate([-(site_total[0:3] + long_force[0:3]), site_energy], axis=0)
     lines = jnp.concatenate([lines, jnp.zeros((4, slots), f32)], axis=0)
-    hot = (iota((slots, slots), 0) == site_of(pos_ref[...])).astype(f32)
-    out_ref[...] = dot(lines, hot, nn, highest)
+    hot = (iota((slots, slots), 0) == site_of(coords_of(pos_ref))).astype(f32).astype(bf16)
+    lines = exact(lines, hot)
+    for axis in range(3):
+        force_out[0, 0, axis] = lines[axis : axis + 1]
+    energy_out[0, 0] = lines[3:4]
 
 
 def kernel_params():
@@ -1102,18 +1164,15 @@
     energy_weight,
 ):
     axes = ("gx", "gy", "gz")
-    coords = positions.reshape(3, slots)
     vmem = pl.BlockSpec(memory_space=pltpu.VMEM)
     smem = pl.BlockSpec(memory_space=pltpu.SMEM)
     placed = pl.pallas_call(
         place_kernel,
-        out_shape=jax.ShapeDtypeStruct((4, slots), f32),
+        out_shape=jax.ShapeDtypeStruct((domains, 4, slots), f32),
         in_specs=[smem, vmem, vmem],
         out_specs=vmem,
-    )(counts.reshape(1), coords, species.reshape(1, slots))
-    shared = lax.all_to_all(
-        jnp.broadcast_to(placed[None], (domains, 4, slots)), axes, 0, 0, tiled=True
-    )
+    )(counts, positions.transpose(0, 1, 3, 2, 4), species)
+    shared = lax.all_to_all(placed, axes, 0, 0, tiled=True)
     prepared = pl.pallas_call(
         weights_kernel,
         out_shape=(
@@ -1124,53 +1183,60 @@
             jax.ShapeDtypeStruct((2, 256, 128), bf16),
             jax.ShapeDtypeStruct((2, 128, 256), bf16),
             jax.ShapeDtypeStruct((2, chan, chan), bf16),
-            jax.ShapeDtypeStruct((16, 256), bf16),
+            jax.ShapeDtypeStruct((half, 256, 128), bf16),
+            jax.ShapeDtypeStruct((8, 128), f32),
         ),
-        in_specs=[vmem] * 8,
-        out_specs=(vmem,) * 8,
+        in_specs=[vmem] * 10,
+        out_specs=(vmem,) * 9,
         compiler_params=kernel_params(),
-    )(kvec, lr_filter, embed, radial_one, radial_two, mix_one, mix_two, read_weight)
+    )(
+        kvec,
+        lr_filter,
+        embed,
+        radial_one,
+        radial_two,
+        mix_one,
+        mix_two,
+        read_weight,
+        read_bias.reshape(1, chan),
+        energy_weight.reshape(1, chan),
+    )
     place = jnp.stack([lax.axis_index(axis) for axis in axes]).astype(jnp.int32)
-    result = box_call(
-        place, shared, coords, prepared, read_bias.reshape(1, chan), energy_weight.reshape(1, chan)
-    )
-    return (result[3].reshape(1, 1, 1, slots), result[:3].reshape(1, 1, 1, 3, slots))
-
-
-def box_call(place, shared, coords, prepared, bias, energy, interpret=False):
+    energies, forces = box_call(place, shared, positions.transpose(0, 1, 3, 2, 4), prepared)
+    return (energies, forces.transpose(0, 1, 3, 2, 4))
+
+
+def box_call(place, shared, coords, prepared):
     vmem = pl.BlockSpec(memory_space=pltpu.VMEM)
     smem = pl.BlockSpec(memory_space=pltpu.SMEM)
     grid_shape = (ext, ext, ext, planes, 128)
     return pl.pallas_call(
         box_kernel,
-        out_shape=jax.ShapeDtypeStruct((8, slots), f32),
-        in_specs=[smem] + [vmem] * 12,
-        out_specs=vmem,
+        out_shape=(
+            jax.ShapeDtypeStruct((1, 1, 1, slots), f32),
+            jax.ShapeDtypeStruct((1, 1, 3, 1, slots), f32),
+        ),
+        in_specs=[smem] + [vmem] * 11,
+        out_specs=(vmem, vmem),
         scratch_shapes=[
             pltpu.VMEM((cells // 128, 64 * 16, 128), f32),
             pltpu.VMEM((64, pad), f32),
             pltpu.VMEM((2, rows_all, 128), f32),
             pltpu.VMEM((half, rows_all, pad), f32),
-            pltpu.VMEM((2, table, planes * pad), bf16),
+            pltpu.VMEM((table, domains * slots), bf16),
             pltpu.VMEM((table, cells), bf16),
             pltpu.VMEM(grid_shape, f32),
             pltpu.VMEM(grid_shape, f32),
             pltpu.VMEM(grid_shape, f32),
-            pltpu.VMEM(grid_shape, f32),
-            pltpu.VMEM((planes * pad, 128), bf16),
-            pltpu.VMEM((cells + 80, 256), f32),
+            pltpu.VMEM((domains * slots, 128), f32),
             pltpu.VMEM((2, pad, 128), f32),
+            pltpu.VMEM((8, domains * slots), f32),
+            pltpu.VMEM((rows_all, pad), bf16),
+            pltpu.VMEM((table, 128), f32),
+            pltpu.VMEM((2, cells, chan), f32),
         ],
         compiler_params=kernel_params(),
-        interpret=interpret,
-    )(
-        place,
-        shared,
-        coords,
-        *prepared,
-        jnp.concatenate([bias, bias], axis=1),
-        jnp.concatenate([energy, energy], axis=1),
-    )
+    )(place, shared, coords, *prepared)
 
 
 def solution(mesh):

time: 66.2 us -> 55.7 us (0.84)
  local copies, waits for them, and re-layouts: 5.73 us -> 0.62 us
  Pallas kernels: 49.2 us -> 44.4 us
  other arithmetic: 2 us -> 0.62 us
  waiting for transfers between devices: 0.16 us -> 1.21 us
    pallas_call x2, Pallas kernels: 44.5 us -> 39.3 us  [the longest x1 37.8 us: box_call(): pl.pallas_call(box_kernel, out_shape=(jax.ShapeDtypeStruct((1, 1, 1, slot...]
    unnamed x4 -> x2, local copies, waits for them, and re-layouts: 2.48 us -> 0.62 us
    concatenate x1 -> x0, other arithmetic: 1.34 us -> none  [box_call(): jnp.concatenate([bias, bias], axis=1)]
    broadcast_in_dim x1 -> x0, local copies, waits for them, and re-layouts: 1.3 us -> none  [whole_box(): jnp.broadcast_to(placed[None], (domains, 4, slots))]
    another operation x1 -> x0, local copies, waits for them, and re-layouts: 1.26 us -> none  [whole_box(): result[3].reshape(1, 1, 1, slots)]
    all_to_all x1, waiting for transfers between devices: 0.16 us -> 1.21 us  [whole_box(): shared = lax.all_to_all(placed, axes, 0, 0, tiled=True)]
    reshape x1 -> x0, local copies, waits for them, and re-layouts: 0.7 us -> none  [whole_box(): result[:3].reshape(1, 1, 1, 3, slots)]
  transfers between devices with their start and end apart: 1 -> 1, of which waited for: 1 -> 1; matrix products, arithmetic and copies ran while one was open for 3% -> 1% of each run, Pallas kernels for 7% -> 9%
where the time goes in v1:
time: 55.7 us; the launch traced here: 55.5 us
  Pallas kernels  44.4 us (80%)
  starting transfers between devices  7.36 us (13%)
  between operations  1.3 us (2%)
  waiting for transfers between devices  1.21 us (2%)
  other arithmetic  0.62 us (1%)
  local copies, waits for them, and re-layouts  0.62 us (1%)
    pallas_call x1, Pallas kernels, box_call(): pl.pallas_call(box_kernel, out_shape=(jax.ShapeDtypeStruct((1, 1, 1, slot...  37.8 us
    all_to_all x1, starting transfers between devices, whole_box(): shared = lax.all_to_all(placed, axes, 0, 0, tiled=True)  7.36 us
    pallas_call x1, Pallas kernels, whole_box(): pl.pallas_call(weights_kernel, out_shape=(jax.ShapeDtypeStruct((table, ch...  5.05 us
    pallas_call x1, Pallas kernels, whole_box(): pl.pallas_call(place_kernel, out_shape=jax.ShapeDtypeStruct((domains, 4,...  1.51 us
    all_to_all x1, waiting for transfers between devices, whole_box(): shared = lax.all_to_all(placed, axes, 0, 0, tiled=True)  1.21 us
  transfers between devices with their start and end apart: 1, of which 1 were waited for; matrix products, arithmetic and copies ran while one was open for 1% of the time, Pallas kernels for 9%

profile of v1, /device:TPU:0, one launch (start us, length us, event | category | flops | bytes accessed | tf_op | source)
XLA Modules:
  0.0 55.5 jit_solution(5811650063162575874)
XLA Ops:
  1.3 1.5 %shard_map.140 = f32[16,4,216]{2,1,0:T(4,128)} custom-call(s32[1,1,1]{2,1,0:T(1,128)S(6)} %copy.16.count_ref, f32[1,1,3,1,216]{4,3,2,1,0:T(1,128)} %bitcast.9, s32[1,1,1,216]{3,2,1,0:T(1,128)} %species_ref.1), custom_call_target="tpu_custom_call" | custom-call | tf_op jit(solution)/shard_map/pallas_call | solution.py:1169
  2.8 7.4 %all-to-all-start = ((f32[16,4,216]{2,1,0:T(4,128)}), f32[16,4,216]{2,1,0:T(4,128)S(1)}, u32[]{:S(2)}, u32[]{:S(2)}) async-start(f32[16,4,216]{2,1,0:T(4,128)} %shard_map.140), calls=%async_computation | async-start | bytes 131072 | tf_op jit(solution)/shard_map/all_to_all | solution.py:1175
  10.2 5.0 %shard_map.141 = (f32[1296,64]{1,0:T(8,128)}, bf16[13,256,256]{2,1,0:T(8,128)(2,1)}, bf16[256,384]{1,0:T(8,128)(2,1)}, bf16[2,128,128]{2,1,0:T(8,128)(2,1)}, bf1...) custom-call(s32[3,4096]{1,0:T(4,128)} %kvec_ref.1, ...), custom_call_target="tpu_custom_call" | custom-call | tf_op jit(solution)/shard_map/pallas_call | solution.py:1176
  15.2 0.6 %pad_add_fusion.place_ref = s32[3]{0:T(128)} fusion(s32[1]{0:T(128)} %bitcast.2, s32[1]{0:T(128)} %bitcast.1, s32[1]{0:T(128)} %bitcast), kind=kLoop, calls=%fused_computation | loop fusion | flops 6 | bytes 24 | tf_op jit(solution)/shard_map/stack | solution.py:1204
  15.8 1.2 %all-to-all-done.all_ref = f32[16,4,216]{2,1,0:T(4,128)S(1)} async-done(((f32[16,4,216]{2,1,0:T(4,128)}), f32[16,4,216]{2,1,0:T(4,128)S(1)}, u32[]{:S(2)}, u32[]{:S(2)}) %all-to-all-start) | async-done | bytes 55328 | tf_op jit(solution)/shard_map/all_to_all | solution.py:1175
  17.0 0.0 copy-start
  17.0 0.6 %copy-done = f32[16,4,216]{2,1,0:T(4,128)} copy-done((f32[16,4,216]{2,1,0:T(4,128)}, f32[16,4,216]{2,1,0:T(4,128)S(1)}, u32[]{:S(2)}) %copy-start) | copy-done | bytes 55320
  17.7 37.8 %shard_map.142 = (f32[1,1,1,216]{3,2,1,0:T(1,128)}, f32[1,1,3,1,216]{4,3,2,1,0:T(1,128)}) custom-call(s32[3]{0:T(128)} %pad_add_fusion.place_ref, f32[16,4,216]{2,1,0:T(4,128)} %copy-done, f32[1,1,3,1,216]{4,3,2,1,0:T(1,128)} %bitcast.10, f32[1296,64]{1,0:T(8,128)} %get-tuple-element.13.gain_ref, bf16[13,256,256]{2,1,0:T(8,128)(2,1)} %get-tuple-element.14.radial_ref, ...), custom_call_target="tpu_custom_call" | custom-call | tf_op jit(solution)/shard_map/pallas_call | solution.py:1213
Async XLA Ops:
  2.8 14.3 %all-to-all-start = ((f32[16,4,216]{2,1,0:T(4,128)}), f32[16,4,216]{2,1,0:T(4,128)S(1)}, u32[]{:S(2)}, u32[]{:S(2)}) async-start(f32[16,4,216]{2,1,0:T(4,128)} %shard_map.140), calls=%async_computation | async-start | bytes 131072 | tf_op jit(solution)/shard_map/all_to_all | solution.py:1175
  17.0 0.6 %copy-start = (f32[16,4,216]{2,1,0:T(4,128)}, f32[16,4,216]{2,1,0:T(4,128)S(1)}, u32[]{:S(2)}) copy-start(f32[16,4,216]{2,1,0:T(4,128)S(1)} %all-to-all-done.all_ref) | copy-start | bytes 165892

commit v2 on v1

--- a/solution.py
+++ b/solution.py
@@ -517,6 +517,7 @@
 ext = SIDE + 2
 cells = ext**3
 inner_lanes = SIDE * ext * ext
+reach = ext * ext + 2 * ext
 chan = 64
 grid_dims = (4, 2, 2)
 domains = 16
@@ -525,6 +526,7 @@
 waves = 648
 table = 2 * waves
 pad = 256
+span = -(-rows_all // 128) * 128
 gamma = (NBASIS / cutoff) ** 2
 step = cutoff / (NBASIS - 1)
 nt = (((1,), (1,)), ((), ()))
@@ -588,28 +590,7 @@
     )
 
 
-def weights_kernel(
-    kvec_ref,
-    filter_ref,
-    embed_ref,
-    one_ref,
-    two_ref,
-    mix_one_ref,
-    mix_two_ref,
-    read_ref,
-    bias_ref,
-    energy_ref,
-    gain_ref,
-    radial_ref,
-    embed_out,
-    mix_ref,
-    act_ref,
-    grad_ref,
-    back_ref,
-    pair_ref,
-    lines_ref,
-):
-    pair_scale = 1.0 / math.sqrt(NEIGH)
+def gain_kernel(kvec_ref, filter_ref, gain_ref):
     wave_scale = 1.0 / math.sqrt(KVEC * slots * domains)
     waves_in = kvec_ref[...]
 
@@ -625,52 +606,7 @@
         hot = (iota((waves, width), 0) == index[:, start : start + width]).astype(f32).astype(bf16)
         gain = gain + dot(hot, parts[:, start : start + width], nt)
     gain = (gain[:, :chan] + gain[:, chan:]).reshape(waves // 8, 8, chan)
-    gain_ref[...] = jnp.concatenate([gain, gain], axis=1).reshape(table, chan)
-
-    centre = step * iota((NBASIS, 1), 0).astype(f32)
-    fall = jnp.exp(-gamma * centre * centre)
-    rows = iota((pad, pad), 0)
-    columns = iota((pad, pad), 1)
-    kept = (rows // 128) == (columns % 128 // chan)
-
-    def spread(block):
-        return jnp.broadcast_to(block[:, None, :], (NBASIS, 16, chan)).reshape(128, chan)
-
-    def wide(left, right):
-        left, right = spread(left), spread(right)
-        line = jnp.concatenate([left, left, right, right], axis=1)
-        return jnp.concatenate([line, line], axis=0)
-
-    radial = wide(one_ref[...] * fall, two_ref[...] * fall)
-    for offset in range(half):
-        radial_ref[offset] = jnp.where(kept & (rows % 16 == offset), radial, 0.0).astype(bf16)
-    table_rows = jnp.concatenate([embed_ref[...], jnp.zeros((2, chan), f32)], axis=0)
-    high = table_rows.astype(bf16).astype(f32)
-    species_rows = kept & (rows % 16 == half)
-    embeds = jnp.where(species_rows, wide(high, table_rows - high), 0.0).astype(bf16)
-    lives = jnp.where(species_rows[:, :128], 1.0, 0.0).astype(bf16)
-    embed_out[...] = jnp.concatenate([embeds, lives], axis=1)
-
-    def put(ref, value):
-        value_high, value_low = split(value)
-        ref[0] = value_high
-        ref[1] = value_low
-
-    bias = bias_ref[...]
-    energy = energy_ref[...]
-    lines_ref[0:1] = jnp.concatenate([bias, bias], axis=1)
-    lines_ref[1:2] = jnp.concatenate([energy, energy], axis=1)
-    mix_two = mix_two_ref[...]
-    read = read_ref[...]
-    both = dot(mix_two, read, nn, highest) * pair_scale
-    put(mix_ref, twice(mix_one_ref[...] * pair_scale))
-    put(act_ref, jnp.concatenate([twice(read), twice(both)], axis=0))
-    put(grad_ref, jnp.concatenate([twice(read.T), twice(both.T)], axis=1))
-    put(back_ref, mix_one_ref[...].T * pair_scale)
-    pairs = jnp.concatenate([two_ref[...], two_ref[...], one_ref[...], one_ref[...]], axis=1)
-    pairs = jnp.broadcast_to(pairs[:, None, :], (NBASIS, 16, 256)).reshape(128, 256).T
-    for offset in range(half):
-        pair_ref[offset] = jnp.where(columns[:, :128] % 16 == offset, pairs, 0.0).astype(bf16)
+    gain_ref[...] = jnp.concatenate([gain, gain], axis=1).reshape(table, chan).T
 
 
 def turn(fraction):
@@ -731,6 +667,7 @@
         for real, imag in fan(level, z_lines):
             store(index, jnp.concatenate([real, imag], axis=0).astype(bf16))
             index += 1
+        yield index
 
 
 def swap_lanes(value):
@@ -777,9 +714,18 @@
         ).reshape(value.shape)
 
 
-def inner_rows(ref):
+def inner_rows(ref, level):
     inner = slice(1, SIDE + 1)
-    return ref[inner, inner, inner].reshape(rows_all, 128)
+    return ref[level + 1, inner, inner].reshape(rows_all // SIDE, 128)
+
+
+def set_level(ref, level, value):
+    inner = slice(1, SIDE + 1)
+    ref[level + 1, inner, inner] = value.reshape(SIDE, SIDE, planes, 128)
+
+
+def level_rows(level):
+    return slice(level * (rows_all // SIDE), (level + 1) * (rows_all // SIDE))
 
 
 def set_inner(ref, value):
@@ -802,10 +748,14 @@
         for (ox, oy), members in groups.items():
             there = [source[x + 1 + ox, y + 1 + oy, z] for z in range(ext)]
             sums = [None] * ext
+            first = pl.multiple_of(line * (SIDE * planes), SIDE * planes)
+            weights = [
+                filters[number, pl.ds(first, SIDE * planes), lanes].astype(f32)
+                for number, _ in members
+            ]
             for z in range(SIDE):
-                for number, oz in members:
-                    first = pl.multiple_of((line * SIDE + z) * planes, planes)
-                    weight = filters[number, pl.ds(first, planes), lanes]
+                for block, (_, oz) in zip(weights, members):
+                    weight = block[z * planes : z * planes + planes]
                     own_sum[z] = own_sum[z] + weight * there[z + 1 + oz]
                     term = weight * own[z]
                     spot = z + 1 + oz
@@ -827,19 +777,32 @@
     fold_ghosts(target)
 
 
+def spread(block):
+    return jnp.broadcast_to(block[:, None, :], (NBASIS, 16, chan)).reshape(128, chan)
+
+
+def wide(left, right):
+    left, right = spread(left), spread(right)
+    line = jnp.concatenate([left, left, right, right], axis=1)
+    return jnp.concatenate([line, line], axis=0)
+
+
+def doubled(ref):
+    return jnp.concatenate([ref[...], ref[...]], axis=1)
+
+
 def box_kernel(
-    place_ref,
     all_ref,
     pos_ref,
     gain_ref,
-    radial_ref,
     embed_ref,
-    mix_ref,
-    act_ref,
-    grad_ref,
-    back_ref,
-    pair_ref,
-    lines_ref,
+    radial_one_ref,
+    radial_two_ref,
+    mix_one_ref,
+    mix_two_ref,
+    read_ref,
+    bias_ref,
+    energy_ref,
     energy_out,
     force_out,
     sep_ref,
@@ -855,11 +818,26 @@
     own_ref,
     flat_ref,
     low_ref,
-    parts_ref,
     saved_ref,
+    radial_ref,
+    shift_ref,
 ):
-    home = [place_ref[axis] for axis in range(3)]
+    home = [lax.axis_index(axis) for axis in ("gx", "gy", "gz")]
+    pair_scale = 1.0 / math.sqrt(NEIGH)
+    fall = jnp.exp(-gamma * jnp.square(step * iota((NBASIS, 1), 0).astype(f32)))
+    rows = iota((pad, pad), 0)
+    columns = iota((pad, pad), 1)
+    kept = (rows // 128) == (columns % 128 // chan)
+    radial_ref[...] = jnp.where(
+        kept, wide(radial_one_ref[...] * fall, radial_two_ref[...] * fall), 0.0
+    )
+    table_rows = jnp.concatenate([embed_ref[...], jnp.zeros((2, chan), f32)], axis=0)
+    table_high = table_rows.astype(bf16).astype(f32)
+    species_rows = kept & (rows % 16 == half)
+    embeds = jnp.where(species_rows, wide(table_high, table_rows - table_high), 0.0).astype(bf16)
+    lives = jnp.where(species_rows[:, :128], 1.0, 0.0).astype(bf16)
     sites_ref[...] = jnp.zeros((4 * domains, pad), f32)
+    flat_ref[...] = jnp.zeros(flat_ref.shape, f32)
     domain_width = SIDE * spacing
     offset_row = iota((4, slots), 0)
     for number in range(domains):
@@ -873,7 +851,7 @@
         moved = jnp.where(
             offset_row == 0, shifts[0], jnp.where(offset_row == 1, shifts[1], shifts[2])
         )
-        start = (number % 2 * planes + number // 2) * slots
+        start = number % 2 * span + number // 2 * slots
         flat_ref[0:4, start : start + slots] = block + moved
     sites = sites_ref[:, 0:slots]
 
@@ -921,6 +899,7 @@
     for number in range(half, 16):
         put_sep(number, grown)
 
+    basis_unroll = 4
     row16 = iota((16, inner_lanes), 0)
 
     def basis_of(domain):
@@ -947,7 +926,12 @@
             ]
         return carry
 
-    lax.fori_loop(0, planes, basis_step, 0)
+    def basis_group(number, carry):
+        for part in range(basis_unroll):
+            basis_step(number * basis_unroll + part, carry)
+        return carry
+
+    lax.fori_loop(0, planes // basis_unroll, basis_group, 0)
 
     basis_low = jnp.concatenate([basis_ref[0], basis_ref[1]], axis=1).astype(bf16)
     low_ref[...] = basis_low
@@ -958,25 +942,34 @@
         def store(index, value):
             waves_ref[index * 16 : index * 16 + 16, pl.ds(start, 128)] = value
 
-        wave_tile([block[axis : axis + 1] for axis in range(3)], store)
+        return wave_tile([block[axis : axis + 1] for axis in range(3)], store)
 
     def wave_step(number, carry):
-        filters_ref[number] = dot(low_ref[...], radial_ref[number])
+        chosen = jnp.where(iota((pad, pad), 0) % 16 == number, radial_ref[...], 0.0)
+        chosen = chosen.astype(bf16)
+        levels = []
         for part in range(2):
-            flat_tile(pl.multiple_of(number * 256 + part * 128, 128))
+            levels.append(flat_tile(pl.multiple_of(number * 256 + part * 128, 128)))
+        rows_each = rows_all // 6
+        for part in range(6):
+            window = slice(part * rows_each, part * rows_each + rows_each)
+            filters_ref[number, window] = dot(low_ref[window], chosen).astype(bf16)
+            for _ in range(3):
+                next(levels[part // 3])
         return carry
 
     lax.fori_loop(0, half, wave_step, 0)
-    flat_tile(half * 256)
+    for tile in range(2 * half, 2 * span // 128):
+        list(flat_tile(tile * 128))
     for tile in range(cells // 128):
         lanes = slice(tile * 128, tile * 128 + 128)
 
         def store(index, value):
             ring_ref[index * 16 : index * 16 + 16, lanes] = value
 
-        wave_tile([own_ext[axis : axis + 1, lanes] for axis in range(3)], store)
-
-    start_values = dot(basis_low, embed_ref[...])
+        list(wave_tile([own_ext[axis : axis + 1, lanes] for axis in range(3)], store))
+
+    start_values = dot(low_ref[...], jnp.concatenate([embeds, lives], axis=1))
     rows_ref = basis_ref.at[0]
     live_ref = basis_ref.at[1]
     live_ref[...] = start_values[:, 256:384]
@@ -991,73 +984,79 @@
         return jnp.concatenate([value[ext * ext :], value[: ext * ext]], axis=0)[:, :chan]
 
     saved_ref[0] = cells_of(zero_ref)
-    first_rows = inner_rows(zero_ref) + live_ref[...] * dot_split(
-        inner_rows(sum_ref), mix_ref[0], mix_ref[1]
-    )
-    set_inner(one_ref, first_rows)
-    rows_ref[...] = first_rows
+    mix_high, mix_low = split(twice(mix_one_ref[...] * pair_scale))
+    for level in range(SIDE):
+        window = level_rows(level)
+        first_rows = inner_rows(zero_ref, level) + live_ref[window] * dot_split(
+            inner_rows(sum_ref, level), mix_high, mix_low
+        )
+        set_level(one_ref, level, first_rows)
+        rows_ref[window] = first_rows
     fill_ghosts(one_ref)
     saved_ref[1] = cells_of(one_ref)
     two_ref = zero_ref
 
-    def pack_rows():
+    def structure():
         for plane in range(planes):
-            value = rows_ref[pl.ds(plane, slots, stride=planes), :]
-            packed_ref[plane * slots : plane * slots + slots] = value
-            packed_ref[rows_all + plane * slots : rows_all + plane * slots + slots] = pltpu.roll(
-                value, chan, 1
-            )
-        tail = 12 * pad
-        parts_ref[...] = dot(waves_ref[:, tail:], packed_ref[tail:].astype(bf16))
-
-    def structure_step(number):
-        start = pl.multiple_of(number * pad, pad)
-        parts_ref[...] = parts_ref[...] + dot(
-            waves_ref[:, pl.ds(start, pad)], packed_ref[pl.ds(start, pad), :].astype(bf16)
-        )
-
-    def structure():
-        return parts_ref[:, :chan] * gain_ref[...]
-
-    pack_rows()
+            packed_ref[plane * slots : plane * slots + slots] = rows_ref[
+                pl.ds(plane, slots, stride=planes), :
+            ]
+        turned = packed_ref[...].T
+        zeros = jnp.zeros((chan, span - rows_all), f32)
+        turned = jnp.concatenate([turned[:chan], zeros, turned[chan:], zeros], axis=1)
+        return dot(turned.astype(bf16), waves_ref[...], nt) * gain_ref[...]
+
+    filtered = structure()
     own_ref[...] = jnp.zeros(own_ref.shape, f32)
     own_ref[0, 0:slots] = rows_ref[pl.ds(0, slots, stride=planes), :]
-    convolve(filters_ref, 1, one_ref, sum_ref, structure_step)
-    filtered = structure()
-    long_rows = dot(filtered.T.astype(bf16), waves_ref[...]).T
+    convolve(filters_ref, 1, one_ref, sum_ref)
+    long_rows = dot(filtered.astype(bf16), waves_ref[...]).T
     for plane in range(planes):
         first = long_rows[plane * slots : plane * slots + slots]
-        second = long_rows[rows_all + plane * slots : rows_all + plane * slots + slots]
+        second = long_rows[span + plane * slots : span + plane * slots + slots]
         rows_ref[pl.ds(plane, slots, stride=planes), :] = jnp.concatenate([first, second], axis=1)
-    joined = jnp.concatenate([inner_rows(one_ref) + rows_ref[...], inner_rows(sum_ref)], axis=1)
-    act = dot_split(joined, act_ref[0], act_ref[1]) + lines_ref[0:1]
-    sig = 1.0 / (1.0 + jnp.exp(-act))
-    weighted = live_ref[...] * lines_ref[1:2] * sig
-    rows_ref[...] = weighted * act
-    own_energy = rows_ref[pl.ds(0, slots, stride=planes), :]
+    read = read_ref[...]
+    both = dot_split(mix_two_ref[...] * pair_scale, *split(read))
+    act_high, act_low = split(jnp.concatenate([twice(read), twice(both)], axis=0))
+    grad_high, grad_low = split(jnp.concatenate([twice(read.T), twice(both.T)], axis=1))
+    bias = doubled(bias_ref)
+    energy = doubled(energy_ref)
+    for level in range(SIDE):
+        window = level_rows(level)
+        joined = jnp.concatenate(
+            [inner_rows(one_ref, level) + rows_ref[window], inner_rows(sum_ref, level)], axis=1
+        )
+        act = dot_split(joined, act_high, act_low) + bias
+        sig = 1.0 / (1.0 + jnp.exp(-act))
+        weighted = live_ref[window] * energy * sig
+        packed_ref[window] = weighted * act
+        grads = dot_split(weighted * (1.0 + act * (1.0 - sig)), grad_high, grad_low)
+        rows_ref[window] = grads[:, :128]
+        set_level(two_ref, level, grads[:, 128:])
+    own_energy = packed_ref[pl.ds(0, slots, stride=planes), :]
     first_half = jnp.where(iota((8, 128), 1) < chan, 1.0, 0.0)
     energy_high, energy_low = split(own_energy)
     first_half = first_half.astype(bf16)
     site_energy = (dot(first_half, energy_high, nt) + dot(first_half, energy_low, nt))[0:1]
-    grads = dot_split(weighted * (1.0 + act * (1.0 - sig)), grad_ref[0], grad_ref[1])
-    rows_ref[...] = grads[:, :128]
-    set_inner(two_ref, grads[:, 128:])
     fill_ghosts(two_ref)
-    pack_rows()
+    back = structure()
     own_ref[1, 0:slots] = rows_ref[pl.ds(0, slots, stride=planes), :]
     two_cells = cells_of(two_ref)
-    convolve(filters_ref, 1, two_ref, sum_ref, structure_step)
-    back = structure()
-    back_rows = back.T.astype(bf16)
-    set_inner(sum_ref, rows_ref[...] + live_ref[...] * inner_rows(sum_ref))
+    convolve(filters_ref, 1, two_ref, sum_ref)
+    back_rows = back.astype(bf16)
+    for level in range(SIDE):
+        window = level_rows(level)
+        set_level(
+            sum_ref, level, rows_ref[window] + live_ref[window] * inner_rows(sum_ref, level)
+        )
     fill_ghosts(sum_ref)
     sum_cells = cells_of(sum_ref)
     live_cells = jnp.where(own_ext[3:4] > 0, 1.0, 0.0)
     ring_long = (dot(back_rows, ring_ref[...]) * live_cells).T
-    grad_cells = dot_split(sum_cells + ring_long, back_ref[0], back_ref[1])
+    grad_cells = dot_split(sum_cells + ring_long, *split(mix_one_ref[...].T * pair_scale))
 
     def crossed(value):
-        value = value.reshape(waves // 8, 2, 8, chan)
+        value = value.T.reshape(waves // 8, 2, 8, chan)
         value = jnp.concatenate([value[:, 1:2], -value[:, 0:1]], axis=1).reshape(table, chan)
         return jnp.concatenate([value, jnp.zeros((table, chan), f32)], axis=1).astype(bf16)
 
@@ -1100,16 +1099,20 @@
         axis=1,
     )
     left = jnp.concatenate(left, axis=1)
-    reach = ext * ext + 2 * ext
     for shift in range(3):
         moved = right if shift == 1 else pltpu.roll(right, (1 - shift) % cells, 0)
-        filters_ref[shift, 0:cells] = moved
-        filters_ref[shift, cells : cells + reach] = moved[:reach]
+        shift_ref[shift, 0:cells] = moved
+        shift_ref[shift, cells:] = moved[:reach]
+    one, two = radial_one_ref[...], radial_two_ref[...]
+    pairs = jnp.concatenate([two, two, one, one], axis=1)
+    pairs = jnp.broadcast_to(pairs[:, None, :], (NBASIS, 16, pad)).reshape(128, pad).T
+    pair_column = iota((pad, 128), 1) % 16
     shares = jnp.zeros((cells, 128), f32)
     for number, (ox, oy, oz) in enumerate(offsets):
         distance = (ox * ext + oy) * ext
-        products = left * filters_ref[oz + 1, distance : distance + cells]
-        shares = shares + dot(products.astype(bf16), pair_ref[number])
+        products = left * shift_ref[oz + 1, distance : distance + cells]
+        chosen = jnp.where(pair_column == number, pairs, 0.0).astype(bf16)
+        shares = shares + dot(products.astype(bf16), chosen)
     shares = shares.T
     sep = [get_sep(slice(16 * part, 16 * part + 16)) for part in range(3)]
     square = sep[0] * sep[0] + sep[1] * sep[1] + sep[2] * sep[2]
@@ -1143,7 +1146,7 @@
 
 
 def kernel_params():
-    return pltpu.CompilerParams(vmem_limit_bytes=63 * 1024 * 1024)
+    return pltpu.CompilerParams(vmem_limit_bytes=56 * 1024 * 1024)
 
 
 def whole_box(
@@ -1173,25 +1176,14 @@
         out_specs=vmem,
     )(counts, positions.transpose(0, 1, 3, 2, 4), species)
     shared = lax.all_to_all(placed, axes, 0, 0, tiled=True)
-    prepared = pl.pallas_call(
-        weights_kernel,
-        out_shape=(
-            jax.ShapeDtypeStruct((table, chan), f32),
-            jax.ShapeDtypeStruct((half, pad, pad), bf16),
-            jax.ShapeDtypeStruct((pad, 384), bf16),
-            jax.ShapeDtypeStruct((2, 128, 128), bf16),
-            jax.ShapeDtypeStruct((2, 256, 128), bf16),
-            jax.ShapeDtypeStruct((2, 128, 256), bf16),
-            jax.ShapeDtypeStruct((2, chan, chan), bf16),
-            jax.ShapeDtypeStruct((half, 256, 128), bf16),
-            jax.ShapeDtypeStruct((8, 128), f32),
-        ),
-        in_specs=[vmem] * 10,
-        out_specs=(vmem,) * 9,
-        compiler_params=kernel_params(),
-    )(
-        kvec,
-        lr_filter,
+    gain = pl.pallas_call(
+        gain_kernel,
+        out_shape=jax.ShapeDtypeStruct((chan, table), f32),
+        in_specs=[vmem] * 2,
+        out_specs=vmem,
+    )(kvec, lr_filter)
+    tables = (
+        gain,
         embed,
         radial_one,
         radial_two,
@@ -1201,14 +1193,12 @@
         read_bias.reshape(1, chan),
         energy_weight.reshape(1, chan),
     )
-    place = jnp.stack([lax.axis_index(axis) for axis in axes]).astype(jnp.int32)
-    energies, forces = box_call(place, shared, positions.transpose(0, 1, 3, 2, 4), prepared)
+    energies, forces = box_call(shared, positions.transpose(0, 1, 3, 2, 4), tables)
     return (energies, forces.transpose(0, 1, 3, 2, 4))
 
 
-def box_call(place, shared, coords, prepared):
+def box_call(shared, coords, tables):
     vmem = pl.BlockSpec(memory_space=pltpu.VMEM)
-    smem = pl.BlockSpec(memory_space=pltpu.SMEM)
     grid_shape = (ext, ext, ext, planes, 128)
     return pl.pallas_call(
         box_kernel,
@@ -1216,27 +1206,28 @@
             jax.ShapeDtypeStruct((1, 1, 1, slots), f32),
             jax.ShapeDtypeStruct((1, 1, 3, 1, slots), f32),
         ),
-        in_specs=[smem] + [vmem] * 11,
+        in_specs=[vmem] * 11,
         out_specs=(vmem, vmem),
         scratch_shapes=[
             pltpu.VMEM((cells // 128, 64 * 16, 128), f32),
             pltpu.VMEM((64, pad), f32),
             pltpu.VMEM((2, rows_all, 128), f32),
-            pltpu.VMEM((half, rows_all, pad), f32),
-            pltpu.VMEM((table, domains * slots), bf16),
+            pltpu.VMEM((half, rows_all, pad), bf16),
+            pltpu.VMEM((table, 2 * span), bf16),
             pltpu.VMEM((table, cells), bf16),
             pltpu.VMEM(grid_shape, f32),
             pltpu.VMEM(grid_shape, f32),
             pltpu.VMEM(grid_shape, f32),
-            pltpu.VMEM((domains * slots, 128), f32),
+            pltpu.VMEM((rows_all, 128), f32),
             pltpu.VMEM((2, pad, 128), f32),
-            pltpu.VMEM((8, domains * slots), f32),
+            pltpu.VMEM((8, 2 * span), f32),
             pltpu.VMEM((rows_all, pad), bf16),
-            pltpu.VMEM((table, 128), f32),
             pltpu.VMEM((2, cells, chan), f32),
+            pltpu.VMEM((pad, pad), f32),
+            pltpu.VMEM((3, cells + reach, 256), f32),
         ],
         compiler_params=kernel_params(),
-    )(place, shared, coords, *prepared)
+    )(shared, coords, *tables)
 
 
 def solution(mesh):

time: 55.7 us -> 51.5 us (0.925)
  Pallas kernels: 44.4 us -> 39 us
  waiting for transfers between devices: 1.21 us -> 3 us
  other arithmetic: 0.62 us -> 0 us
    pallas_call x1, Pallas kernels: 37.8 us -> 33.6 us  [box_call(): pl.pallas_call(box_kernel, out_shape=(jax.ShapeDtypeStruct((1, 1, 1, slot...]
    all_to_all x1, waiting for transfers between devices: 1.21 us -> 3 us  [whole_box(): shared = lax.all_to_all(placed, axes, 0, 0, tiled=True)]
    pallas_call x1, Pallas kernels: 5.05 us -> 3.9 us  [whole_box(): pl.pallas_call(gain_kernel, out_shape=jax.ShapeDtypeStruct((chan, table),...]
    another operation x1 -> x0, other arithmetic: 0.62 us -> none  [whole_box(): place = jnp.stack([lax.axis_index(axis) for axis in axes]).astype(jnp.int32)]
  transfers between devices with their start and end apart: 1 -> 1, of which waited for: 1 -> 1; matrix products, arithmetic and copies ran while one was open for 1% -> 0% of each run, Pallas kernels for 9% -> 8%
where the time goes in v2:
time: 51.5 us; the launch traced here: 51.3 us
  Pallas kernels  39 us (76%)
  starting transfers between devices  7.36 us (14%)
  waiting for transfers between devices  3 us (6%)
  between operations  1.29 us (3%)
  local copies, waits for them, and re-layouts  0.62 us (1%)
    pallas_call x1, Pallas kernels, box_call(): pl.pallas_call(box_kernel, out_shape=(jax.ShapeDtypeStruct((1, 1, 1, slot...  33.6 us
    all_to_all x1, starting transfers between devices, whole_box(): shared = lax.all_to_all(placed, axes, 0, 0, tiled=True)  7.36 us
    pallas_call x1, Pallas kernels, whole_box(): pl.pallas_call(gain_kernel, out_shape=jax.ShapeDtypeStruct((chan, table),...  3.9 us
    all_to_all x1, waiting for transfers between devices, whole_box(): shared = lax.all_to_all(placed, axes, 0, 0, tiled=True)  3 us
    pallas_call x1, Pallas kernels, whole_box(): pl.pallas_call(place_kernel, out_shape=jax.ShapeDtypeStruct((domains, 4,...  1.51 us
  transfers between devices with their start and end apart: 1, of which 1 were waited for; matrix products, arithmetic and copies ran while one was open for 0% of the time, Pallas kernels for 8%

profile of v2, /device:TPU:0, one launch (start us, length us, event | category | flops | bytes accessed | tf_op | source)
XLA Modules:
  0.0 51.3 jit_solution(801694465243721576)
XLA Ops:
  1.3 1.5 %shard_map.140 = f32[16,4,216]{2,1,0:T(4,128)} custom-call(s32[1,1,1]{2,1,0:T(1,128)S(6)} %copy.16.count_ref, f32[1,1,3,1,216]{4,3,2,1,0:T(1,128)} %bitcast.6, s32[1,1,1,216]{3,2,1,0:T(1,128)} %species_ref.1), custom_call_target="tpu_custom_call" | custom-call | tf_op jit(solution)/shard_map/pallas_call | solution.py:1172
  2.8 7.4 %all-to-all-start = ((f32[16,4,216]{2,1,0:T(4,128)}), f32[16,4,216]{2,1,0:T(4,128)S(1)}, u32[]{:S(2)}, u32[]{:S(2)}) async-start(f32[16,4,216]{2,1,0:T(4,128)} %shard_map.140), calls=%async_computation | async-start | bytes 131072 | tf_op jit(solution)/shard_map/all_to_all | solution.py:1178
  10.1 3.9 %shard_map.141.gain_ref = f32[64,1296]{1,0:T(8,128)} custom-call(s32[3,4096]{1,0:T(4,128)} %kvec_ref.1, f32[64,4096]{1,0:T(8,128)} %filter_ref.1), custom_call_target="tpu_custom_call" | custom-call | tf_op jit(solution)/shard_map/pallas_call | solution.py:1179
  14.0 3.0 %all-to-all-done.all_ref = f32[16,4,216]{2,1,0:T(4,128)S(1)} async-done(((f32[16,4,216]{2,1,0:T(4,128)}), f32[16,4,216]{2,1,0:T(4,128)S(1)}, u32[]{:S(2)}, u32[]{:S(2)}) %all-to-all-start) | async-done | bytes 55328 | tf_op jit(solution)/shard_map/all_to_all | solution.py:1178
  17.0 0.0 copy-start
  17.0 0.6 %copy-done = f32[16,4,216]{2,1,0:T(4,128)} copy-done((f32[16,4,216]{2,1,0:T(4,128)}, f32[16,4,216]{2,1,0:T(4,128)S(1)}, u32[]{:S(2)}) %copy-start) | copy-done | bytes 55320
  17.7 33.6 %shard_map.142 = (f32[1,1,1,216]{3,2,1,0:T(1,128)}, f32[1,1,3,1,216]{4,3,2,1,0:T(1,128)}) custom-call(f32[16,4,216]{2,1,0:T(4,128)} %copy-done, f32[1,1,3,1,216]{4,3,2,1,0:T(1,128)} %bitcast.7, f32[64,1296]{1,0:T(8,128)} %shard_map.141.gain_ref, f32[6,64]{1,0:T(8,128)} %embed_ref.1, f32[8,64]{1,0:T(8,128)} %radial_one_ref.1, f32[8,64]{1,0:T(8,128)} %radial_two_ref.1, ...), custom_call_target="tpu_custom_call" | custom-call | tf_op jit(solution)/shard_map/pallas_call | solution.py:1203
Async XLA Ops:
  2.8 14.3 %all-to-all-start = ((f32[16,4,216]{2,1,0:T(4,128)}), f32[16,4,216]{2,1,0:T(4,128)S(1)}, u32[]{:S(2)}, u32[]{:S(2)}) async-start(f32[16,4,216]{2,1,0:T(4,128)} %shard_map.140), calls=%async_computation | async-start | bytes 131072 | tf_op jit(solution)/shard_map/all_to_all | solution.py:1178
  17.0 0.6 %copy-start = (f32[16,4,216]{2,1,0:T(4,128)}, f32[16,4,216]{2,1,0:T(4,128)S(1)}, u32[]{:S(2)}) copy-start(f32[16,4,216]{2,1,0:T(4,128)S(1)} %all-to-all-done.all_ref) | copy-start | bytes 165892

commit v3 on v2

--- a/solution.py
+++ b/solution.py
@@ -767,10 +767,11 @@
             target[x + 1, y + 1, z + 1] = target[x + 1, y + 1, z + 1] + own_sum[z]
 
     def body(number, carry):
+        one_line(number * 3)
         if beside is not None:
             beside(number)
-        for part in range(3):
-            one_line(number * 3 + part)
+        one_line(number * 3 + 1)
+        one_line(number * 3 + 2)
         return carry
 
     lax.fori_loop(0, SIDE * SIDE // 3, body, 0)
@@ -821,6 +822,8 @@
     saved_ref,
     radial_ref,
     shift_ref,
+    turned_ref,
+    parts_ref,
 ):
     home = [lax.axis_index(axis) for axis in ("gx", "gy", "gz")]
     pair_scale = 1.0 / math.sqrt(NEIGH)
@@ -899,7 +902,7 @@
     for number in range(half, 16):
         put_sep(number, grown)
 
-    basis_unroll = 4
+    basis_unroll = 8
     row16 = iota((16, inner_lanes), 0)
 
     def basis_of(domain):
@@ -996,7 +999,7 @@
     saved_ref[1] = cells_of(one_ref)
     two_ref = zero_ref
 
-    def structure():
+    def start_structure():
         for plane in range(planes):
             packed_ref[plane * slots : plane * slots + slots] = rows_ref[
                 pl.ds(plane, slots, stride=planes), :
@@ -1004,12 +1007,21 @@
         turned = packed_ref[...].T
         zeros = jnp.zeros((chan, span - rows_all), f32)
         turned = jnp.concatenate([turned[:chan], zeros, turned[chan:], zeros], axis=1)
-        return dot(turned.astype(bf16), waves_ref[...], nt) * gain_ref[...]
-
-    filtered = structure()
+        turned_ref[...] = turned.astype(bf16)
+        tail = 12 * pad
+        parts_ref[...] = dot(turned_ref[:, tail:], waves_ref[:, tail:], nt)
+
+    def step_structure(number):
+        start = pl.multiple_of(number * pad, pad)
+        parts_ref[...] = parts_ref[...] + dot(
+            turned_ref[:, pl.ds(start, pad)], waves_ref[:, pl.ds(start, pad)], nt
+        )
+
+    start_structure()
     own_ref[...] = jnp.zeros(own_ref.shape, f32)
     own_ref[0, 0:slots] = rows_ref[pl.ds(0, slots, stride=planes), :]
-    convolve(filters_ref, 1, one_ref, sum_ref)
+    convolve(filters_ref, 1, one_ref, sum_ref, step_structure)
+    filtered = parts_ref[...] * gain_ref[...]
     long_rows = dot(filtered.astype(bf16), waves_ref[...]).T
     for plane in range(planes):
         first = long_rows[plane * slots : plane * slots + slots]
@@ -1039,10 +1051,11 @@
     first_half = first_half.astype(bf16)
     site_energy = (dot(first_half, energy_high, nt) + dot(first_half, energy_low, nt))[0:1]
     fill_ghosts(two_ref)
-    back = structure()
+    start_structure()
     own_ref[1, 0:slots] = rows_ref[pl.ds(0, slots, stride=planes), :]
     two_cells = cells_of(two_ref)
-    convolve(filters_ref, 1, two_ref, sum_ref)
+    convolve(filters_ref, 1, two_ref, sum_ref, step_structure)
+    back = parts_ref[...] * gain_ref[...]
     back_rows = back.astype(bf16)
     for level in range(SIDE):
         window = level_rows(level)
@@ -1225,6 +1238,8 @@
             pltpu.VMEM((2, cells, chan), f32),
             pltpu.VMEM((pad, pad), f32),
             pltpu.VMEM((3, cells + reach, 256), f32),
+            pltpu.VMEM((chan, 2 * span), bf16),
+            pltpu.VMEM((chan, table), f32),
         ],
         compiler_params=kernel_params(),
     )(shared, coords, *tables)

time: 51.5 us -> 49.7 us (0.965)
  Pallas kernels: 39 us -> 37.1 us
    pallas_call x1, Pallas kernels: 33.6 us -> 31.7 us  [box_call(): pl.pallas_call(box_kernel, out_shape=(jax.ShapeDtypeStruct((1, 1, 1, slot...]
where the time goes in v3:
time: 49.7 us; the launch traced here: 49.4 us
  Pallas kernels  37.1 us (75%)
  starting transfers between devices  7.36 us (15%)
  waiting for transfers between devices  3 us (6%)
  between operations  1.29 us (3%)
  local copies, waits for them, and re-layouts  0.62 us (1%)
    pallas_call x1, Pallas kernels, box_call(): pl.pallas_call(box_kernel, out_shape=(jax.ShapeDtypeStruct((1, 1, 1, slot...  31.7 us
    all_to_all x1, starting transfers between devices, whole_box(): shared = lax.all_to_all(placed, axes, 0, 0, tiled=True)  7.36 us
    pallas_call x1, Pallas kernels, whole_box(): pl.pallas_call(gain_kernel, out_shape=jax.ShapeDtypeStruct((chan, table),...  3.9 us
    all_to_all x1, waiting for transfers between devices, whole_box(): shared = lax.all_to_all(placed, axes, 0, 0, tiled=True)  3 us
    pallas_call x1, Pallas kernels, whole_box(): pl.pallas_call(place_kernel, out_shape=jax.ShapeDtypeStruct((domains, 4,...  1.51 us
  transfers between devices with their start and end apart: 1, of which 1 were waited for; matrix products, arithmetic and copies ran while one was open for 0% of the time, Pallas kernels for 8%

profile of v3, /device:TPU:0, one launch (start us, length us, event | category | flops | bytes accessed | tf_op | source)
XLA Modules:
  0.0 49.4 jit_solution(10615957967959656315)
XLA Ops:
  1.3 1.5 %shard_map.140 = f32[16,4,216]{2,1,0:T(4,128)} custom-call(s32[1,1,1]{2,1,0:T(1,128)S(6)} %copy.16.count_ref, f32[1,1,3,1,216]{4,3,2,1,0:T(1,128)} %bitcast.6, s32[1,1,1,216]{3,2,1,0:T(1,128)} %species_ref.1), custom_call_target="tpu_custom_call" | custom-call | tf_op jit(solution)/shard_map/pallas_call | solution.py:1185
  2.8 7.4 %all-to-all-start = ((f32[16,4,216]{2,1,0:T(4,128)}), f32[16,4,216]{2,1,0:T(4,128)S(1)}, u32[]{:S(2)}, u32[]{:S(2)}) async-start(f32[16,4,216]{2,1,0:T(4,128)} %shard_map.140), calls=%async_computation | async-start | bytes 131072 | tf_op jit(solution)/shard_map/all_to_all | solution.py:1191
  10.1 3.9 %shard_map.141.gain_ref = f32[64,1296]{1,0:T(8,128)} custom-call(s32[3,4096]{1,0:T(4,128)} %kvec_ref.1, f32[64,4096]{1,0:T(8,128)} %filter_ref.1), custom_call_target="tpu_custom_call" | custom-call | tf_op jit(solution)/shard_map/pallas_call | solution.py:1192
  14.0 3.0 %all-to-all-done.all_ref = f32[16,4,216]{2,1,0:T(4,128)S(1)} async-done(((f32[16,4,216]{2,1,0:T(4,128)}), f32[16,4,216]{2,1,0:T(4,128)S(1)}, u32[]{:S(2)}, u32[]{:S(2)}) %all-to-all-start) | async-done | bytes 55328 | tf_op jit(solution)/shard_map/all_to_all | solution.py:1191
  17.0 0.0 copy-start
  17.0 0.6 %copy-done = f32[16,4,216]{2,1,0:T(4,128)} copy-done((f32[16,4,216]{2,1,0:T(4,128)}, f32[16,4,216]{2,1,0:T(4,128)S(1)}, u32[]{:S(2)}) %copy-start) | copy-done | bytes 55320
  17.7 31.7 %shard_map.142 = (f32[1,1,1,216]{3,2,1,0:T(1,128)}, f32[1,1,3,1,216]{4,3,2,1,0:T(1,128)}) custom-call(f32[16,4,216]{2,1,0:T(4,128)} %copy-done, f32[1,1,3,1,216]{4,3,2,1,0:T(1,128)} %bitcast.7, f32[64,1296]{1,0:T(8,128)} %shard_map.141.gain_ref, f32[6,64]{1,0:T(8,128)} %embed_ref.1, f32[8,64]{1,0:T(8,128)} %radial_one_ref.1, f32[8,64]{1,0:T(8,128)} %radial_two_ref.1, ...), custom_call_target="tpu_custom_call" | custom-call | tf_op jit(solution)/shard_map/pallas_call | solution.py:1216
Async XLA Ops:
  2.8 14.3 %all-to-all-start = ((f32[16,4,216]{2,1,0:T(4,128)}), f32[16,4,216]{2,1,0:T(4,128)S(1)}, u32[]{:S(2)}, u32[]{:S(2)}) async-start(f32[16,4,216]{2,1,0:T(4,128)} %shard_map.140), calls=%async_computation | async-start | bytes 131072 | tf_op jit(solution)/shard_map/all_to_all | solution.py:1191
  17.0 0.6 %copy-start = (f32[16,4,216]{2,1,0:T(4,128)}, f32[16,4,216]{2,1,0:T(4,128)S(1)}, u32[]{:S(2)}) copy-start(f32[16,4,216]{2,1,0:T(4,128)S(1)} %all-to-all-done.all_ref) | copy-start | bytes 165892

commit v4 on v3

--- a/solution.py
+++ b/solution.py
@@ -767,14 +767,13 @@
             target[x + 1, y + 1, z + 1] = target[x + 1, y + 1, z + 1] + own_sum[z]
 
     def body(number, carry):
-        one_line(number * 3)
-        if beside is not None:
-            beside(number)
-        one_line(number * 3 + 1)
-        one_line(number * 3 + 2)
+        for part in range(6):
+            one_line(number * 6 + part)
+            if beside is not None and part % 3 == 0:
+                beside(number * 2 + part // 3)
         return carry
 
-    lax.fori_loop(0, SIDE * SIDE // 3, body, 0)
+    lax.fori_loop(0, SIDE, body, 0)
     fold_ghosts(target)
 
 

time: 49.7 us -> 47.7 us (0.960)
  Pallas kernels: 37.1 us -> 35.2 us
    pallas_call x1, Pallas kernels: 31.7 us -> 29.8 us  [box_call(): pl.pallas_call(box_kernel, out_shape=(jax.ShapeDtypeStruct((1, 1, 1, slot...]
where the time goes in v4:
time: 47.7 us; the launch traced here: 47.5 us
  Pallas kernels  35.2 us (74%)
  starting transfers between devices  7.36 us (15%)
  waiting for transfers between devices  3 us (6%)
  between operations  1.29 us (3%)
  local copies, waits for them, and re-layouts  0.62 us (1%)
    pallas_call x1, Pallas kernels, box_call(): pl.pallas_call(box_kernel, out_shape=(jax.ShapeDtypeStruct((1, 1, 1, slot...  29.8 us
    all_to_all x1, starting transfers between devices, whole_box(): shared = lax.all_to_all(placed, axes, 0, 0, tiled=True)  7.36 us
    pallas_call x1, Pallas kernels, whole_box(): pl.pallas_call(gain_kernel, out_shape=jax.ShapeDtypeStruct((chan, table),...  3.9 us
    all_to_all x1, waiting for transfers between devices, whole_box(): shared = lax.all_to_all(placed, axes, 0, 0, tiled=True)  3 us
    pallas_call x1, Pallas kernels, whole_box(): pl.pallas_call(place_kernel, out_shape=jax.ShapeDtypeStruct((domains, 4,...  1.51 us
  transfers between devices with their start and end apart: 1, of which 1 were waited for; matrix products, arithmetic and copies ran while one was open for 0% of the time, Pallas kernels for 8%

profile of v4, /device:TPU:0, one launch (start us, length us, event | category | flops | bytes accessed | tf_op | source)
XLA Modules:
  0.0 47.5 jit_solution(4669357542886136224)
XLA Ops:
  1.3 1.5 %shard_map.140 = f32[16,4,216]{2,1,0:T(4,128)} custom-call(s32[1,1,1]{2,1,0:T(1,128)S(6)} %copy.16.count_ref, f32[1,1,3,1,216]{4,3,2,1,0:T(1,128)} %bitcast.6, s32[1,1,1,216]{3,2,1,0:T(1,128)} %species_ref.1), custom_call_target="tpu_custom_call" | custom-call | tf_op jit(solution)/shard_map/pallas_call | solution.py:1184
  2.8 7.4 %all-to-all-start = ((f32[16,4,216]{2,1,0:T(4,128)}), f32[16,4,216]{2,1,0:T(4,128)S(1)}, u32[]{:S(2)}, u32[]{:S(2)}) async-start(f32[16,4,216]{2,1,0:T(4,128)} %shard_map.140), calls=%async_computation | async-start | bytes 131072 | tf_op jit(solution)/shard_map/all_to_all | solution.py:1190
  10.1 3.9 %shard_map.141.gain_ref = f32[64,1296]{1,0:T(8,128)} custom-call(s32[3,4096]{1,0:T(4,128)} %kvec_ref.1, f32[64,4096]{1,0:T(8,128)} %filter_ref.1), custom_call_target="tpu_custom_call" | custom-call | tf_op jit(solution)/shard_map/pallas_call | solution.py:1191
  14.0 3.0 %all-to-all-done.all_ref = f32[16,4,216]{2,1,0:T(4,128)S(1)} async-done(((f32[16,4,216]{2,1,0:T(4,128)}), f32[16,4,216]{2,1,0:T(4,128)S(1)}, u32[]{:S(2)}, u32[]{:S(2)}) %all-to-all-start) | async-done | bytes 55328 | tf_op jit(solution)/shard_map/all_to_all | solution.py:1190
  17.0 0.0 copy-start
  17.0 0.6 %copy-done = f32[16,4,216]{2,1,0:T(4,128)} copy-done((f32[16,4,216]{2,1,0:T(4,128)}, f32[16,4,216]{2,1,0:T(4,128)S(1)}, u32[]{:S(2)}) %copy-start) | copy-done | bytes 55320
  17.7 29.8 %shard_map.142 = (f32[1,1,1,216]{3,2,1,0:T(1,128)}, f32[1,1,3,1,216]{4,3,2,1,0:T(1,128)}) custom-call(f32[16,4,216]{2,1,0:T(4,128)} %copy-done, f32[1,1,3,1,216]{4,3,2,1,0:T(1,128)} %bitcast.7, f32[64,1296]{1,0:T(8,128)} %shard_map.141.gain_ref, f32[6,64]{1,0:T(8,128)} %embed_ref.1, f32[8,64]{1,0:T(8,128)} %radial_one_ref.1, f32[8,64]{1,0:T(8,128)} %radial_two_ref.1, ...), custom_call_target="tpu_custom_call" | custom-call | tf_op jit(solution)/shard_map/pallas_call | solution.py:1215
Async XLA Ops:
  2.8 14.3 %all-to-all-start = ((f32[16,4,216]{2,1,0:T(4,128)}), f32[16,4,216]{2,1,0:T(4,128)S(1)}, u32[]{:S(2)}, u32[]{:S(2)}) async-start(f32[16,4,216]{2,1,0:T(4,128)} %shard_map.140), calls=%async_computation | async-start | bytes 131072 | tf_op jit(solution)/shard_map/all_to_all | solution.py:1190
  17.0 0.6 %copy-start = (f32[16,4,216]{2,1,0:T(4,128)}, f32[16,4,216]{2,1,0:T(4,128)S(1)}, u32[]{:S(2)}) copy-start(f32[16,4,216]{2,1,0:T(4,128)S(1)} %all-to-all-done.all_ref) | copy-start | bytes 165892

commit v5 on v4

--- a/solution.py
+++ b/solution.py
@@ -773,7 +773,7 @@
                 beside(number * 2 + part // 3)
         return carry
 
-    lax.fori_loop(0, SIDE, body, 0)
+    lax.fori_loop(0, SIDE * SIDE // 6, body, 0)
     fold_ghosts(target)
 
 
@@ -952,12 +952,12 @@
         levels = []
         for part in range(2):
             levels.append(flat_tile(pl.multiple_of(number * 256 + part * 128, 128)))
-        rows_each = rows_all // 6
-        for part in range(6):
+        rows_each = rows_all // 3
+        for part in range(3):
             window = slice(part * rows_each, part * rows_each + rows_each)
             filters_ref[number, window] = dot(low_ref[window], chosen).astype(bf16)
-            for _ in range(3):
-                next(levels[part // 3])
+            for turn_number in range(6):
+                next(levels[(part * 6 + turn_number) // 9])
         return carry
 
     lax.fori_loop(0, half, wave_step, 0)

time: 47.7 us -> 47.6 us (level)
  no operation moved by 1% of the time
where the time goes in v5:
time: 47.6 us; the launch traced here: 47.3 us
  Pallas kernels  35.1 us (74%)
  starting transfers between devices  7.36 us (15%)
  waiting for transfers between devices  3 us (6%)
  between operations  1.29 us (3%)
  local copies, waits for them, and re-layouts  0.62 us (1%)
    pallas_call x1, Pallas kernels, box_call(): pl.pallas_call(box_kernel, out_shape=(jax.ShapeDtypeStruct((1, 1, 1, slot...  29.7 us
    all_to_all x1, starting transfers between devices, whole_box(): shared = lax.all_to_all(placed, axes, 0, 0, tiled=True)  7.36 us
    pallas_call x1, Pallas kernels, whole_box(): pl.pallas_call(gain_kernel, out_shape=jax.ShapeDtypeStruct((chan, table),...  3.9 us
    all_to_all x1, waiting for transfers between devices, whole_box(): shared = lax.all_to_all(placed, axes, 0, 0, tiled=True)  3 us
    pallas_call x1, Pallas kernels, whole_box(): pl.pallas_call(place_kernel, out_shape=jax.ShapeDtypeStruct((domains, 4,...  1.51 us
  transfers between devices with their start and end apart: 1, of which 1 were waited for; matrix products, arithmetic and copies ran while one was open for 0% of the time, Pallas kernels for 8%

profile of v5, /device:TPU:0, one launch (start us, length us, event | category | flops | bytes accessed | tf_op | source)
XLA Modules:
  0.0 47.3 jit_solution(13688515793867785653)
XLA Ops:
  1.3 1.5 %shard_map.140 = f32[16,4,216]{2,1,0:T(4,128)} custom-call(s32[1,1,1]{2,1,0:T(1,128)S(6)} %copy.16.count_ref, f32[1,1,3,1,216]{4,3,2,1,0:T(1,128)} %bitcast.6, s32[1,1,1,216]{3,2,1,0:T(1,128)} %species_ref.1), custom_call_target="tpu_custom_call" | custom-call | tf_op jit(solution)/shard_map/pallas_call | solution.py:1184
  2.8 7.4 %all-to-all-start = ((f32[16,4,216]{2,1,0:T(4,128)}), f32[16,4,216]{2,1,0:T(4,128)S(1)}, u32[]{:S(2)}, u32[]{:S(2)}) async-start(f32[16,4,216]{2,1,0:T(4,128)} %shard_map.140), calls=%async_computation | async-start | bytes 131072 | tf_op jit(solution)/shard_map/all_to_all | solution.py:1190
  10.1 3.9 %shard_map.141.gain_ref = f32[64,1296]{1,0:T(8,128)} custom-call(s32[3,4096]{1,0:T(4,128)} %kvec_ref.1, f32[64,4096]{1,0:T(8,128)} %filter_ref.1), custom_call_target="tpu_custom_call" | custom-call | tf_op jit(solution)/shard_map/pallas_call | solution.py:1191
  14.0 3.0 %all-to-all-done.all_ref = f32[16,4,216]{2,1,0:T(4,128)S(1)} async-done(((f32[16,4,216]{2,1,0:T(4,128)}), f32[16,4,216]{2,1,0:T(4,128)S(1)}, u32[]{:S(2)}, u32[]{:S(2)}) %all-to-all-start) | async-done | bytes 55328 | tf_op jit(solution)/shard_map/all_to_all | solution.py:1190
  17.0 0.0 copy-start
  17.0 0.6 %copy-done = f32[16,4,216]{2,1,0:T(4,128)} copy-done((f32[16,4,216]{2,1,0:T(4,128)}, f32[16,4,216]{2,1,0:T(4,128)S(1)}, u32[]{:S(2)}) %copy-start) | copy-done | bytes 55320
  17.7 29.7 %shard_map.142 = (f32[1,1,1,216]{3,2,1,0:T(1,128)}, f32[1,1,3,1,216]{4,3,2,1,0:T(1,128)}) custom-call(f32[16,4,216]{2,1,0:T(4,128)} %copy-done, f32[1,1,3,1,216]{4,3,2,1,0:T(1,128)} %bitcast.7, f32[64,1296]{1,0:T(8,128)} %shard_map.141.gain_ref, f32[6,64]{1,0:T(8,128)} %embed_ref.1, f32[8,64]{1,0:T(8,128)} %radial_one_ref.1, f32[8,64]{1,0:T(8,128)} %radial_two_ref.1, ...), custom_call_target="tpu_custom_call" | custom-call | tf_op jit(solution)/shard_map/pallas_call | solution.py:1215
Async XLA Ops:
  2.8 14.3 %all-to-all-start = ((f32[16,4,216]{2,1,0:T(4,128)}), f32[16,4,216]{2,1,0:T(4,128)S(1)}, u32[]{:S(2)}, u32[]{:S(2)}) async-start(f32[16,4,216]{2,1,0:T(4,128)} %shard_map.140), calls=%async_computation | async-start | bytes 131072 | tf_op jit(solution)/shard_map/all_to_all | solution.py:1190
  17.0 0.6 %copy-start = (f32[16,4,216]{2,1,0:T(4,128)}, f32[16,4,216]{2,1,0:T(4,128)S(1)}, u32[]{:S(2)}) copy-start(f32[16,4,216]{2,1,0:T(4,128)S(1)} %all-to-all-done.all_ref) | copy-start | bytes 165892
